TPU v7x, 512 devices: a whole 4x4x16 slice. The times are simulated.
512 devices in a mesh: dp: 4 (over y), sp: 16 (over z_lo, core), tp: 8 (over z_hi, x).
Axes of the slice: x: 4, y: 4, z: 16 (z_hi: 2, z_lo: 8; z = z_hi * 8 + z_lo), core: 2. Of those that a mesh axis runs over, the one named last changes fastest.
Arguments:
- spatial_input: bfloat16 [4, 16, 256, 1152], P('dp', 'sp'), may hold values from -7 to 7
- out_grad: bfloat16 [4, 16, 256, 1152], P('dp', 'sp'), may hold values from -0.75 to 0.75
- qkv_spatial: bfloat16 [1152, 3, 1152], P(None, None, 'tp'), may hold values from -0.1875 to 0.1875
- out_spatial: bfloat16 [1152, 1152], P('tp'), may hold values from -0.1875 to 0.1875
- qkv_temporal: bfloat16 [1152, 3, 1152], P(None, None, 'tp'), may hold values from -0.1875 to 0.1875
- out_temporal: bfloat16 [1152, 1152], P('tp'), may hold values from -0.1875 to 0.1875
Outputs:
- input_grad: bfloat16 [4, 16, 256, 1152], P('dp', 'sp')
- qkv_spatial_grad: float32 [1152, 3, 1152], P(('sp', 'dp'), None, 'tp')
- out_spatial_grad: float32 [1152, 1152], P('tp', ('sp', 'dp'))
- qkv_temporal_grad: float32 [1152, 3, 1152], P(('sp', 'dp'), None, 'tp')
- out_temporal_grad: float32 [1152, 1152], P('tp', ('sp', 'dp'))
All inputs are finite; a program needn't handle non-finite values.
Results may differ from a plain program's by a relative error of at most 0.035.
Values may be sent and summed in bfloat16 or wider, within the bound.
A program may use at most 64 MiB of HBM per device.

v0:
```python
import jax
import jax.numpy as jnp
from jax import lax
from jax.sharding import PartitionSpec as P

HEAD_DIM = 72


def contract_rows(left_rows, right_rows):
    return lax.dot_general(
        left_rows, right_rows, (((0,), (0,)), ((), ())), preferred_element_type=jnp.float32
    )


def times_transpose(left_rows, weight):
    return lax.dot_general(
        left_rows, weight, (((1,), (1,)), ((), ())), preferred_element_type=jnp.float32
    )


def project(tokens, weight):
    token_rows = tokens.reshape(-1, tokens.shape[-1])
    flat_rows = jnp.dot(
        token_rows, weight.reshape(weight.shape[0], -1), preferred_element_type=jnp.float32
    )
    packed = flat_rows.astype(jnp.bfloat16).reshape(
        tokens.shape[0], tokens.shape[1], 3, -1, HEAD_DIM
    )
    return (packed[:, :, 0], packed[:, :, 1], packed[:, :, 2])


def attend(queries, key_rows, value_rows):
    factor = HEAD_DIM ** (-0.5)
    scores = (
        jnp.einsum("blhe,bmhe->bhlm", queries, key_rows, preferred_element_type=jnp.float32)
        * factor
    )
    softmax_rows = jax.nn.softmax(scores, axis=-1)
    weights = softmax_rows.astype(jnp.bfloat16)
    mixed_rows = jnp.einsum(
        "bhlm,bmhe->blhe", weights, value_rows, preferred_element_type=jnp.float32
    )
    return (softmax_rows, weights, mixed_rows.astype(jnp.bfloat16))


def attend_back(queries, key_rows, value_rows, softmax_rows, weights, grad_mixed):
    factor = HEAD_DIM ** (-0.5)
    grad_values = jnp.einsum(
        "bhlm,blhe->bmhe", weights, grad_mixed, preferred_element_type=jnp.float32
    )
    grad_probs = jnp.einsum(
        "blhe,bmhe->bhlm", grad_mixed, value_rows, preferred_element_type=jnp.float32
    )
    centre = jnp.sum(grad_probs * softmax_rows, axis=-1, keepdims=True)
    grad_scores = (softmax_rows * (grad_probs - centre) * factor).astype(jnp.bfloat16)
    grad_queries = jnp.einsum(
        "bhlm,bmhe->blhe", grad_scores, key_rows, preferred_element_type=jnp.float32
    )
    grad_keys = jnp.einsum(
        "bhlm,blhe->bmhe", grad_scores, queries, preferred_element_type=jnp.float32
    )
    return jnp.stack([grad_queries, grad_keys, grad_values], axis=2).astype(jnp.bfloat16)


def heads_total(partial_value):
    return lax.psum(partial_value.astype(jnp.bfloat16), "tp").astype(jnp.float32)


def to_temporal(first_part, second_part):
    return (
        lax.all_to_all(first_part, "sp", split_axis=2, concat_axis=1, tiled=True),
        lax.all_to_all(second_part, "sp", split_axis=2, concat_axis=1, tiled=True),
    )


def to_spatial(first_part, second_part):
    return (
        lax.all_to_all(first_part, "sp", split_axis=1, concat_axis=2, tiled=True),
        lax.all_to_all(second_part, "sp", split_axis=1, concat_axis=2, tiled=True),
    )


def on_device(spatial_input, out_grad, qkv_spatial, out_spatial, qkv_temporal, out_temporal):
    videos, frames_dev, patches, model_width = spatial_input.shape
    frames = frames_dev * lax.axis_size("sp")
    patches_dev = patches // lax.axis_size("sp")
    head_cols = out_temporal.shape[0]
    sequences = spatial_input.reshape(videos * frames_dev, patches, model_width)
    queries, key_rows, value_rows = project(sequences, qkv_spatial)
    softmax_s, weights_s, mixed_s = attend(queries, key_rows, value_rows)
    flat_s = mixed_s.reshape(videos * frames_dev * patches, -1)
    partial_value = jnp.dot(flat_s, out_spatial, preferred_element_type=jnp.float32).reshape(
        spatial_input.shape
    )
    mixed_input = (spatial_input.astype(jnp.float32) + heads_total(partial_value)).astype(
        jnp.bfloat16
    )
    temporal_in, temporal_out_grad = to_temporal(mixed_input, out_grad)
    temporal_seq = temporal_in.transpose(0, 2, 1, 3).reshape(
        videos * patches_dev, frames, model_width
    )
    queries_t, key_rows_t, value_rows_t = project(temporal_seq, qkv_temporal)
    softmax_t, weights_t, mixed_t = attend(queries_t, key_rows_t, value_rows_t)
    grad_rows = temporal_out_grad.transpose(0, 2, 1, 3).reshape(-1, model_width)
    grad_mixed_t = (
        times_transpose(grad_rows, out_temporal).astype(jnp.bfloat16).reshape(mixed_t.shape)
    )
    grads_t = attend_back(queries_t, key_rows_t, value_rows_t, softmax_t, weights_t, grad_mixed_t)
    flat_grads_t = grads_t.reshape(videos * patches_dev * frames, -1)
    qkv_t_term = contract_rows(temporal_seq.reshape(-1, model_width), flat_grads_t).reshape(
        qkv_temporal.shape
    )
    back_t = times_transpose(flat_grads_t, qkv_temporal.reshape(model_width, -1))
    back_t = back_t.reshape(videos, patches_dev, frames, model_width).transpose(0, 2, 1, 3)
    mixed_t_layout = mixed_t.reshape(videos, patches_dev, frames, head_cols).transpose(0, 2, 1, 3)
    mixed_grad = (temporal_out_grad.astype(jnp.float32) + heads_total(back_t)).astype(jnp.bfloat16)
    temporal_grad, mixed_t_frames = to_spatial(mixed_grad, mixed_t_layout)
    out_t_term = contract_rows(
        mixed_t_frames.reshape(-1, head_cols), out_grad.reshape(-1, model_width)
    )
    spatial_rows = temporal_grad.reshape(-1, model_width)
    grad_mixed_s = (
        times_transpose(spatial_rows, out_spatial).astype(jnp.bfloat16).reshape(mixed_s.shape)
    )
    grads_s = attend_back(queries, key_rows, value_rows, softmax_s, weights_s, grad_mixed_s)
    flat_grads_s = grads_s.reshape(spatial_rows.shape[0], -1)
    out_s_term = contract_rows(flat_s, spatial_rows)
    qkv_s_term = contract_rows(spatial_input.reshape(-1, model_width), flat_grads_s).reshape(
        qkv_spatial.shape
    )
    back_s = times_transpose(flat_grads_s, qkv_spatial.reshape(model_width, -1)).reshape(
        spatial_input.shape
    )
    input_grad = (temporal_grad.astype(jnp.float32) + heads_total(back_s)).astype(jnp.bfloat16)
    frame_sums = (
        lax.psum_scatter(
            qkv_s_term.astype(jnp.bfloat16), "sp", scatter_dimension=0, tiled=True
        ).astype(jnp.float32),
        lax.psum_scatter(
            out_s_term.astype(jnp.bfloat16), "sp", scatter_dimension=1, tiled=True
        ).astype(jnp.float32),
        lax.psum_scatter(
            qkv_t_term.astype(jnp.bfloat16), "sp", scatter_dimension=0, tiled=True
        ).astype(jnp.float32),
        lax.psum_scatter(
            out_t_term.astype(jnp.bfloat16), "sp", scatter_dimension=1, tiled=True
        ).astype(jnp.float32),
    )
    video_sums = (
        lax.psum_scatter(
            frame_sums[0].astype(jnp.bfloat16), "dp", scatter_dimension=0, tiled=True
        ).astype(jnp.float32),
        lax.psum_scatter(
            frame_sums[1].astype(jnp.bfloat16), "dp", scatter_dimension=1, tiled=True
        ).astype(jnp.float32),
        lax.psum_scatter(
            frame_sums[2].astype(jnp.bfloat16), "dp", scatter_dimension=0, tiled=True
        ).astype(jnp.float32),
        lax.psum_scatter(
            frame_sums[3].astype(jnp.bfloat16), "dp", scatter_dimension=1, tiled=True
        ).astype(jnp.float32),
    )
    return (input_grad, video_sums[0], video_sums[1], video_sums[2], video_sums[3])


def solution(mesh):
    placed = (
        P("dp", "sp", None, None),
        P("dp", "sp", None, None),
        P(None, None, "tp"),
        P("tp", None),
        P(None, None, "tp"),
        P("tp", None),
    )
    return jax.shard_map(
        on_device,
        mesh=mesh,
        in_specs=placed,
        out_specs=(
            P("dp", "sp", None, None),
            P(("sp", "dp"), None, "tp"),
            P("tp", ("sp", "dp")),
            P(("sp", "dp"), None, "tp"),
            P("tp", ("sp", "dp")),
        ),
        check_vma=False,
    )
```

profile of v0, /device:TPU:6, one launch (start us, length us, event | category | flops | bytes accessed | tf_op | source)
XLA Modules:
  0.0 1137.2 jit_solution(8021297918284467997)
XLA Ops:
  7.2 2.1 copy.195
  9.8 4.4 reduce.6
  14.2 1.0 reshape.285
  15.1 12.6 %all-to-all-start = ((bf16[16,2,9216]{2,1,0:T(2,128)(2,1)}), bf16[16,2,9216]{2,1,0:T(2,128)(2,1)S(1)}, u32[]{:S(2)}, u32[]{:S(2)}) async-start(bf16[16,2,9216]{2,1,0:T(2,128)(2,1)} %reshape.285), calls=%async_computation | async-start | bytes 1179648 | tf_op jit(solution)/shard_map/all_to_all | solution.py:72
  28.5 1.2 fusion.60
  30.7 1.2 fusion.4
  31.9 154.0 %all-reduce.12.cloned.1.call-done = bf16[1,1,256,1152]{3,2,1,0:T(8,128)(2,1)} async-done(((bf16[1,1,256,1152]{3,2,1,0:T(8,128)(2,1)}), bf16[1,1,256,1152]{3,2,1,0:T(8,128)(2,1)}) %all-reduce.12.cloned.1.call-update) | async-done | bytes 589840 | tf_op jit(solution)/shard_map/psum | solution.py:66
  185.8 1.2 add_convert_fusion.1
  187.1 0.9 copy.194
  188.0 5.2 reduce.7
  193.2 2.5 reshape.287
  195.6 3.6 all-to-all-start.1
  199.3 2.2 reshape.286
  203.0 24.2 %all-to-all-done.1 = bf16[16,2,9216]{2,1,0:T(2,128)(2,1)S(1)} async-done(((bf16[16,2,9216]{2,1,0:T(2,128)(2,1)}), bf16[16,2,9216]{2,1,0:T(2,128)(2,1)S(1)}, u32[]{:S(2)}, u32[]{:S(2)}) %all-to-all-start.1) | async-done | bytes 589856 | tf_op jit(solution)/shard_map/all_to_all | solution.py:71
  230.7 1.3 convolution_bitcast_fusion.1
  232.7 1.3 fusion.5
  235.2 7.9 all-to-all-start.3
  243.1 145.5 %all-reduce.14.cloned.1.call-done = bf16[1,16,16,1152]{3,1,2,0:T(8,128)(2,1)} async-done(((bf16[1,16,16,1152]{3,1,2,0:T(8,128)(2,1)}), bf16[1,16,16,1152]{3,1,2,0:T(8,128)(2,1)}) %all-reduce.14.cloned.1.call-update) | async-done | bytes 589840 | tf_op jit(solution)/shard_map/psum | solution.py:66
  388.6 1.2 add_convert_fusion
  389.8 0.9 copy.126
  390.8 4.2 all-to-all-start.2
  395.4 1.1 copy.157
  397.6 9.1 copy.153
  406.7 2.4 reshape.272
  409.1 14.2 %all-to-all-done.2 = bf16[1,16,16,1152]{3,2,0,1:T(8,128)(2,1)} async-done(((bf16[1,16,16,1152]{3,2,0,1:T(8,128)(2,1)}), bf16[1,16,16,1152]{3,2,0,1:T(8,128)(2,1)}, u32[]{:S(2)}, u32[]{:S(2)}) %all-to-all-start.2) | async-done | bytes 589856 | tf_op jit(solution)/shard_map/all_to_all | solution.py:78
  423.3 1.3 convolution_convert_fusion.6
  424.6 1.1 copy.149
  425.7 1.4 convolution_convert_fusion.10
  427.5 1.5 fusion.21
  429.0 1.6 fusion.22
  432.1 3.2 copy.131
  435.4 1.1 copy-done.4
  436.5 1.3 fusion.6
  438.0 1.3 dynamic-slice.2
  439.2 1.3 dynamic-slice
  441.8 61.4 %reduce-scatter.17.cloned.1.call-done = bf16[72,144]{1,0:T(8,128)(2,1)} async-done(((bf16[1152,144]{1,0:T(8,128)(2,1)}), bf16[72,144]{1,0:T(8,128)(2,1)}) %reduce-scatter.17.cloned.1.call-update) | async-done | bytes 20752
  503.2 1.5 copy.158
  504.7 101.7 %reduce-scatter.15.cloned.1.call-done = bf16[72,432]{1,0:T(8,128)(2,1)} async-done(((bf16[1152,432]{1,0:T(8,128)(2,1)}), bf16[72,432]{1,0:T(8,128)(2,1)}) %reduce-scatter.15.cloned.1.call-update) | async-done | bytes 62224
  606.4 1.0 reshape.273
  608.1 100.1 %reduce-scatter.13.cloned.1.call-done = bf16[72,144]{1,0:T(8,128)(2,1)} async-done(((bf16[1152,144]{1,0:T(8,128)(2,1)}), bf16[72,144]{1,0:T(8,128)(2,1)}) %reduce-scatter.13.cloned.1.call-update) | async-done | bytes 20752
  708.1 1.5 copy.150
  709.6 201.9 %all-reduce.18.cloned.1.call-done = bf16[1152,3,144]{2,1,0:T(4,128)(2,1)} async-done(((bf16[1152,3,144]{2,1,0:T(4,128)(2,1)}), bf16[1152,3,144]{2,1,0:T(4,128)(2,1)}) %all-reduce.18.cloned.1.call-update) | async-done | bytes 995344
  911.6 1.6 constant_dynamic-slice_fusion
  913.2 158.2 %all-reduce.16.cloned.1.call-done = bf16[1,1,256,1152]{3,2,1,0:T(8,128)(2,1)} async-done(((bf16[1,1,256,1152]{3,2,1,0:T(8,128)(2,1)}), bf16[1,1,256,1152]{3,2,1,0:T(8,128)(2,1)}) %all-reduce.16.cloned.1.call-update) | async-done | bytes 589840 | tf_op jit(solution)/shard_map/psum | solution.py:66
  1071.4 2.2 fusion.14
  1073.6 51.6 %all-reduce.20.cloned.1.call-done = (bf16[72,3,144]{2,1,0:T(4,128)(2,1)}, bf16[144,72]{1,0:T(8,128)(2,1)}, bf16[72,3,144]{2,0,1:T(8,128)(2,1)}, bf16[144,72]{1,0:T(8,128)(2,1)}) async-done(((bf16[72,3,144]{2,1,0:T(4,128)(2,1)}, bf16[144,72]{1,0:T(8,128)(2,1)}, bf16[72,3,144]{2,0,1:T(8,128)(2,1)}, bf16[144,72]{1,0:T(8,128)(2,1)}), (bf16[72,3,144]{2,1,0:T(4,128)(2,1)}, bf16[144,72]{1,0:T(8,128)(2,1)}, ...) | async-done | bytes 165904
  1125.2 1.4 dynamic-slice_convert_fusion.3
  1128.1 0.9 dynamic-slice_convert_fusion
  (88 shorter events, 16.0 us)
Async XLA Ops:
  7.2 220.8 %copy-start = (bf16[1152,3,144]{0,2,1:T(8,128)(2,1)S(1)}, bf16[1152,3,144]{0,2,1:T(8,128)(2,1)}, u32[]{:S(2)}) copy-start(bf16[1152,3,144]{0,2,1:T(8,128)(2,1)} %param.10) | copy-start | bytes 2985988
  14.1 13.8 %copy-start.1 = (bf16[1,1,256,1152]{3,2,1,0:T(8,128)(2,1)S(1)}, bf16[1,1,256,1152]{3,2,1,0:T(8,128)(2,1)}, u32[]{:S(2)}) copy-start(bf16[1,1,256,1152]{3,2,1,0:T(8,128)(2,1)} %param.6) | copy-start | bytes 1769476
  14.1 13.8 %copy-start.3 = (bf16[1152,3,144]{0,2,1:T(8,128)(2,1)S(1)}, bf16[1152,3,144]{0,2,1:T(8,128)(2,1)}, u32[]{:S(2)}) copy-start(bf16[1152,3,144]{0,2,1:T(8,128)(2,1)} %param.8) | copy-start | bytes 2985988
  15.1 180.5 %all-to-all-start = ((bf16[16,2,9216]{2,1,0:T(2,128)(2,1)}), bf16[16,2,9216]{2,1,0:T(2,128)(2,1)S(1)}, u32[]{:S(2)}, u32[]{:S(2)}) async-start(bf16[16,2,9216]{2,1,0:T(2,128)(2,1)} %reshape.285), calls=%async_computation | async-start | bytes 1179648 | tf_op jit(solution)/shard_map/all_to_all | solution.py:72
  27.7 158.1 %all-reduce.12.cloned.1.call-start = ((), (), s32[]{:S(2)}) async-start(), calls=%async_computation.7 | async-start | bytes 1179648 | tf_op jit(solution)/shard_map/psum | solution.py:66
  28.5 1.7 copy-start.9
  29.7 1.0 copy-start.7
  30.2 155.6 %copy-start.12 = (bf16[2,72,256]{2,1,0:T(8,128)(2,1)}, bf16[2,72,256]{2,1,0:T(8,128)(2,1)S(1)}, u32[]{:S(2)}) copy-start(bf16[2,72,256]{2,1,0:T(8,128)(2,1)S(1)} %convolution_convert_fusion.15) | copy-start | bytes 221188
  195.6 3.6 copy-start.5
  195.6 31.6 %all-to-all-start.1 = ((bf16[16,2,9216]{2,1,0:T(2,128)(2,1)}), bf16[16,2,9216]{2,1,0:T(2,128)(2,1)S(1)}, u32[]{:S(2)}, u32[]{:S(2)}) async-start(bf16[16,2,9216]{2,1,0:T(2,128)(2,1)} %reshape.287), calls=%async_computation.1 | async-start | bytes 1179648 | tf_op jit(solution)/shard_map/all_to_all | solution.py:71
  199.2 189.4 %all-reduce.14.cloned.1.call-start = ((), (), s32[]{:S(2)}) async-start(), calls=%async_computation.8 | async-start | bytes 1179648 | tf_op jit(solution)/shard_map/psum | solution.py:66
  201.5 1.0 copy-start.11
  229.8 0.7 copy-start.14
  232.7 1.4 copy-start.15
  235.2 155.6 %all-to-all-start.3 = ((bf16[1,16,16,144]{3,2,0,1:T(8,128)(2,1)}), bf16[1,16,16,144]{3,2,0,1:T(8,128)(2,1)S(1)}, u32[]{:S(2)}, u32[]{:S(2)}) async-start(bf16[1,16,16,144]{3,2,0,1:T(8,128)(2,1)} %copy.137), calls=%async_computation.3 | async-start | bytes 262144 | tf_op jit(solution)/shard_map/all_to_all | solution.py:79
  389.8 5.2 copy-start.6
  390.8 32.5 %all-to-all-start.2 = ((bf16[1,16,16,1152]{3,2,0,1:T(8,128)(2,1)}), bf16[1,16,16,1152]{3,2,0,1:T(8,128)(2,1)}, u32[]{:S(2)}, u32[]{:S(2)}) async-start(bf16[1,16,16,1152]{3,2,0,1:T(8,128)(2,1)} %copy.126), calls=%async_computation.2 | async-start | bytes 1179648 | tf_op jit(solution)/shard_map/all_to_all | solution.py:78
  395.0 108.2 %reduce-scatter.17.cloned.1.call-start = ((), (), s32[]{:S(2)}) async-start(), calls=%async_computation.12 | async-start | bytes 626688
  396.5 209.9 %reduce-scatter.15.cloned.1.call-start = ((), (), s32[]{:S(2)}) async-start(), calls=%async_computation.11 | async-start | bytes 1253376
  409.0 14.3 %copy-start.13 = (bf16[2,72,256]{2,1,0:T(8,128)(2,1)S(1)}, bf16[2,72,256]{2,1,0:T(8,128)(2,1)}, u32[]{:S(2)}) copy-start(bf16[2,72,256]{2,1,0:T(8,128)(2,1)} %copy-done.12) | copy-start | bytes 221188
  409.1 16.6 %copy-start.8 = (bf16[144,1152]{1,0:T(8,128)(2,1)S(1)}, bf16[144,1152]{1,0:T(8,128)(2,1)}, u32[]{:S(2)}) copy-start(bf16[144,1152]{1,0:T(8,128)(2,1)} %param.9) | copy-start | bytes 995332
  409.1 299.1 %reduce-scatter.13.cloned.1.call-start = ((), (), s32[]{:S(2)}) async-start(), calls=%async_computation.10 | async-start | bytes 626688
  424.6 2.5 copy-start.10
  427.4 484.1 %all-reduce.18.cloned.1.call-start = ((), (), s32[]{:S(2)}) async-start(), calls=%async_computation.13 | async-start | bytes 4718592
  430.6 1.1 copy-start.2
  435.3 1.2 copy-start.4
  435.4 636.0 %all-reduce.16.cloned.1.call-start = ((), (), s32[]{:S(2)}) async-start(), calls=%async_computation.9 | async-start | bytes 1179648 | tf_op jit(solution)/shard_map/psum | solution.py:66
  437.9 687.3 %all-reduce.20.cloned.1.call-start = ((), (), s32[]{:S(2)}) async-start(), calls=%async_computation.14 | async-start | bytes 663552
Sparse Core Ops, SparseCore 0:
  32.0 153.7 all-reduce.11
  234.2 154.4 all-reduce.13
  398.6 104.4 reduce-scatter.16
  506.1 100.2 reduce-scatter.14
  609.3 98.8 reduce-scatter.12
  710.9 200.5 all-reduce.17
  915.1 156.2 all-reduce.15
  1074.5 50.5 all-reduce.19
where the time goes:
time: 1140 us
  waiting for transfers between devices  1010 us (89%)
  local copies, waits for them, and re-layouts  44.7 us (4%)
  starting transfers between devices  28.9 us (3%)
  other arithmetic  17.4 us (2%)
  matrix products  17.4 us (2%)
  between operations  15.9 us (1%)
    unnamed x13, waiting for transfers between devices  517 us
    psum x3, waiting for transfers between devices, heads_total(): lax.psum(partial_value.astype(jnp.bfloat16), 'tp').astype(jnp.float32)  458 us
    unnamed x54, local copies, waits for them, and re-layouts  36.4 us
    all_to_all x1, waiting for transfers between devices, to_temporal(): lax.all_to_all(first_part, 'sp', split_axis=2, concat_axis=1, tiled=True)  24.2 us
  transfers between devices with their start and end apart: 12, of which 10 were waited for; matrix products, arithmetic and copies ran while one was open for 5% of the time, Pallas kernels for 0%

commit v1 on v0

v1 whole, which is shorter than its diff:
```python
import functools

import jax
import jax.numpy as jnp
import numpy as np
from jax import lax
from jax.experimental import pallas as pl
from jax.experimental.pallas import tpu as pltpu
from jax.sharding import PartitionSpec as P

HEAD_DIM = 72
LANES = 128
ROWS = 16
MESH = pl.DeviceIdType.MESH
F32, BF16 = jnp.float32, jnp.bfloat16


def dot_nn(left, right):
    return lax.dot_general(left, right, (((1,), (0,)), ((), ())), preferred_element_type=F32)


def dot_nt(left, right):
    return lax.dot_general(left, right, (((1,), (1,)), ((), ())), preferred_element_type=F32)


def dot_tn(left, right):
    return lax.dot_general(left, right, (((0,), (0,)), ((), ())), preferred_element_type=F32)


class Sizes:
    def __init__(self, mesh_shape, tokens, width):
        self.ny, self.ns = mesh_shape["dp"], mesh_shape["sp"]
        self.nx = mesh_shape["tp"] // 2
        self.nzl = self.ns // 2
        self.tokens, self.width = tokens, width
        self.tiles = width // LANES
        self.reg = self.tiles // self.nx
        assert self.tiles == self.reg * self.nx + 1
        self.per = self.ns // self.nx
        self.cols = 2 * HEAD_DIM
        self.wide = -(-(4 * self.cols) // LANES) * LANES
        self.core_rows = width // 2
        self.y_rows = self.core_rows // self.ny
        self.rr = width // (self.ns * self.ny)
        self.rp = -(-self.rr // 16) * 16


def row_order(z):
    order = np.arange(z.width).reshape(z.nzl, 2, z.ny, z.rr).transpose(1, 2, 0, 3).reshape(-1)
    onehot = np.zeros((z.width, z.width), np.float32)
    onehot[np.arange(z.width), order] = 1.0
    return onehot.astype(jnp.bfloat16)


def row_pad(z):
    onehot = np.zeros((z.nzl * z.rp, z.y_rows), np.float32)
    for chip in range(z.nzl):
        for row in range(z.rr):
            onehot[chip * z.rp + row, chip * z.rr + row] = 1.0
    return onehot.astype(jnp.bfloat16)


def kernel(
    z,
    x_ref, go_ref, ws_ref, wos_ref, wt_ref, wot_ref, order_ref, pad_ref,
    out_ref, wt_out, ws_out,
    qkv_s, qkv_t, prob_s, prob_t, mix_s, mix_t, gm_t, grads,
    pb, rx, sb, zb, ze, eb,
    ti, tie, tig, tg, tge, tgg, got, ge, geg,
    lt_x, lt_ti, lt_go, lt_tg,
    term, term_in, yb, yr, zw, zr,
    rx_s, rx_r, zb_s, zb_r, ag_s, ag_r, go_s, go_r, gag_s, gag_r, eb_s, eb_r,
    w_s, w_r,
):
    n = z.tokens
    cols = z.cols
    factor = HEAD_DIM ** (-0.5)
    dp, s, t = lax.axis_index("dp"), lax.axis_index("sp"), lax.axis_index("tp")
    zh, xi = t // z.nx, t % z.nx
    zl, core = s // 2, s % 2
    owner = s % z.nx
    is_owner = xi == owner
    last = pl.ds((z.tiles - 1) * LANES, LANES)

    def at_x(k):
        return (dp, s, zh * z.nx + (xi + k + 1) % z.nx)

    def at_z(i):
        place = (zh * z.ns + s + i) % (2 * z.ns)
        return place % z.ns, (dp, place % z.ns, (place // z.ns) * z.nx + xi)

    def send(src, dst, ssem, rsem, dev):
        pltpu.make_async_remote_copy(
            src_ref=src, dst_ref=dst, send_sem=ssem, recv_sem=rsem, device_id=dev, device_id_type=MESH
        ).start()

    def wait(ref, sem):
        pltpu.make_async_copy(ref, ref, sem).wait()

    def tile_lanes(who, j, count=1):
        return pl.ds(pl.multiple_of((who * z.reg + j) * LANES, LANES), count * LANES)

    def rows_of(i, base=0):
        return pl.ds(pl.multiple_of(base + i * ROWS, ROWS), ROWS)

    barrier = pltpu.get_barrier_semaphore()
    for k in range(z.nx - 1):
        pl.semaphore_signal(barrier, inc=1, device_id=at_x(k), device_id_type=MESH)
    for k in range(z.ny - 1):
        pl.semaphore_signal(barrier, inc=1, device_id=((dp + k + 1) % z.ny, s, t), device_id_type=MESH)

    def greet(i, carry):
        pl.semaphore_signal(barrier, inc=1, device_id=at_z(i)[1], device_id_type=MESH)
        return carry

    lax.fori_loop(1, 2 * z.ns, greet, 0)
    pl.semaphore_wait(barrier, (z.nx - 1) + (z.ny - 1) + (2 * z.ns - 1))

    def send_go(i, carry):
        to = (s + i) % z.ns
        send(
            go_ref.at[rows_of(to), tile_lanes(xi, 0, z.reg)],
            got.at[rows_of(s), tile_lanes(xi, 0, z.reg)],
            go_s.at[0], go_r.at[0], (dp, to, t),
        )
        return carry

    def send_go_last(i, carry):
        to = (s + i) % z.ns
        send(go_ref.at[rows_of(to), last], ge.at[rows_of(s // z.nx)], go_s.at[1], go_r.at[1], (dp, to, t))
        return carry

    pltpu.make_async_copy(
        go_ref.at[rows_of(s), tile_lanes(xi, 0, z.reg)], got.at[rows_of(s), tile_lanes(xi, 0, z.reg)], go_r.at[0]
    ).start()
    lax.fori_loop(1, z.ns, send_go, 0)

    @pl.when(is_owner)
    def _():
        pltpu.make_async_copy(go_ref.at[rows_of(s), last], ge.at[rows_of(s // z.nx)], go_r.at[1]).start()
        lax.fori_loop(1, z.ns, send_go_last, 0)

    first_head = lax.broadcasted_iota(jnp.int32, (n, cols), 1) < HEAD_DIM

    def one_head(rows, h):
        keep = first_head if h == 0 else jnp.logical_not(first_head)
        return jnp.where(keep, rows.astype(F32), 0.0).astype(BF16)

    def both_heads(pair):
        return jnp.where(first_head, pair[0], pair[1])

    def project(rows, weight_ref, qkv_ref):
        for part in range(3):
            qkv_ref[part] = dot_nt(rows, weight_ref[part * cols : (part + 1) * cols, :]).astype(BF16)

    def attend(qkv_ref, prob_ref, mix_ref, same):
        q, k, v = qkv_ref[0], qkv_ref[1], qkv_ref[2]
        mixed = []
        for h in range(2):
            scores = dot_nt(one_head(q, h), k) * factor
            if same is not None:
                scores = jnp.where(same, scores, -1e30)
            e = jnp.exp(scores - jnp.max(scores, axis=-1, keepdims=True))
            probs = e / jnp.sum(e, axis=-1, keepdims=True)
            prob_ref[h] = probs
            mixed.append(dot_nn(probs.astype(BF16), v))
        mix_ref[...] = both_heads(mixed).astype(BF16)

    def attend_back(qkv_ref, prob_ref, grad_mixed, grads_ref):
        q, k, v = qkv_ref[0], qkv_ref[1], qkv_ref[2]
        dq, dk, dv = [], [], []
        for h in range(2):
            probs = prob_ref[h]
            dp_ = dot_nt(one_head(grad_mixed, h), v)
            centre = jnp.sum(dp_ * probs, axis=-1, keepdims=True)
            ds = (probs * (dp_ - centre) * factor).astype(BF16)
            dq.append(dot_nn(ds, k))
            dk.append(dot_tn(ds, q))
            dv.append(dot_tn(probs.astype(BF16), grad_mixed))
        for part, pair in enumerate((dq, dk, dv)):
            grads_ref[part] = both_heads(pair).astype(BF16)

    def transposed(rows_ref, lt_ref):
        step = 192 if z.width % 192 == 0 else 160

        def one(i, carry):
            at = pl.ds(pl.multiple_of(i * step, 16), step)
            lt_ref[at, :] = dot_nt(order_ref[at, :], rows_ref[...]).astype(BF16)
            return carry

        lax.fori_loop(0, z.width // step, one, 0)

    def send_x(p, j):
        for k in range(z.nx - 1):
            to = (xi + k + 1) % z.nx
            send(pb.at[p, :, tile_lanes(to, j)], rx.at[p, j, k], rx_s.at[p, j], rx_r.at[p, j], at_x(k))

    def send_x_last(p):
        @pl.when(jnp.logical_not(is_owner))
        def _():
            k = (owner - xi - 1 + z.nx) % z.nx
            send(
                pb.at[p, :, last], rx.at[p, z.reg, k], rx_s.at[p, z.reg], rx_r.at[p, z.reg],
                (dp, s, zh * z.nx + owner),
            )

    def partial_and_send(p, product):
        for j in range(z.reg):
            for who in range(z.nx):
                lanes = slice((who * z.reg + j) * LANES, (who * z.reg + j + 1) * LANES)
                pb[p, :, lanes] = product(lanes).astype(BF16)
            send_x(p, j)
        lanes = slice((z.tiles - 1) * LANES, z.tiles * LANES)
        pb[p, :, lanes] = product(lanes).astype(BF16)
        send_x_last(p)

    def sum_x(p, j, extra=None):
        wait(rx.at[p, j], rx_r.at[p, j])
        lanes = tile_lanes(xi, j) if j < z.reg else last
        total = pb[p, :, lanes].astype(F32)
        for k in range(z.nx - 1):
            total += rx[p, j, k].astype(F32)
        if extra is not None:
            total += extra(lanes)
        sb[p, j] = total.astype(BF16)

    def send_z(p, j):
        if j < z.reg:
            pltpu.make_async_copy(sb.at[p, j, rows_of(s)], zb.at[p, j, rows_of(s, zh * n)], zb_r.at[p, j]).start()
        else:
            pltpu.make_async_copy(
                sb.at[p, j, rows_of(s)], ze.at[p, rows_of(s // z.nx, zh * z.per * ROWS)], zb_r.at[p, j]
            ).start()

        def one(i, carry):
            to, dev = at_z(i)
            dst = zb.at[p, j, rows_of(s, zh * n)] if j < z.reg else ze.at[p, rows_of(s // z.nx, zh * z.per * ROWS)]
            send(sb.at[p, j, rows_of(to)], dst, zb_s.at[p, j], zb_r.at[p, j], dev)
            return carry

        lax.fori_loop(1, 2 * z.ns, one, 0)

    def switch(p, extra=None):
        for j in range(z.reg):
            sum_x(p, j, extra)
            send_z(p, j)

        @pl.when(is_owner)
        def _():
            sum_x(p, z.reg, extra)
            send_z(p, z.reg)

    def sum_z(p, full, mine, others, extra=None):
        for j in range(z.reg):
            wait(zb.at[p, j], zb_r.at[p, j])
            lanes = tile_lanes(xi, j)
            total = zb[p, j, 0:n].astype(F32) + zb[p, j, n : 2 * n].astype(F32)
            if extra is not None:
                total += extra[:, lanes].astype(F32)
            full[:, lanes] = total.astype(BF16)
            for k in range(z.nx - 1):
                send(full.at[:, lanes], full.at[:, lanes], ag_s.at[p, j], ag_r.at[p, j, k], at_x(k))
        wait(ze.at[p], zb_r.at[p, z.reg])
        half = z.per * ROWS
        for i in range(z.per):
            total = ze[p, i * ROWS : (i + 1) * ROWS].astype(F32)
            total += ze[p, half + i * ROWS : half + (i + 1) * ROWS].astype(F32)
            if extra is not None:
                total += extra[rows_of(xi + z.nx * i), last].astype(F32)
            mine[i * ROWS : (i + 1) * ROWS, :] = total.astype(BF16)
        for k in range(z.nx - 1):
            send(mine, others.at[k], ag_s.at[p, z.reg], ag_r.at[p, z.reg, k], at_x(k))

    def place_last(full, block, who):
        for i in range(z.per):
            full[rows_of(who + z.nx * i), last] = block[i * ROWS : (i + 1) * ROWS, :]

    def gather_x(p, full, mine, others):
        place_last(full, mine, xi)
        for k in range(z.nx - 1):
            who = (xi - k - 1 + z.nx) % z.nx
            for j in range(z.reg):
                wait(full.at[:, tile_lanes(who, j)], ag_r.at[p, j, k])
            wait(others.at[k], ag_r.at[p, z.reg, k])
            place_last(full, others.at[k], who)

    def weight_terms(b, lt_qkv, lt_out, mix_ref):
        tail = z.wide - LANES * (3 * cols // LANES)
        base = z.wide - tail
        packed = jnp.concatenate(
            [grads[b, 0], grads[b, 1], grads[b, 2], jnp.zeros((n, z.wide - 3 * cols), BF16)], axis=1
        )
        placed = jnp.concatenate(
            [jnp.zeros((n, 3 * cols - base), BF16), mix_ref[...], jnp.zeros((n, z.wide - 4 * cols), BF16)], axis=1
        )
        step = 192 if z.width % 192 == 0 else 160

        def one(i, carry):
            at = pl.ds(pl.multiple_of(i * step, 16), step)
            left, left_out = lt_qkv[at, :], lt_out[at, :]
            term[b, at, 0:base] = dot_nn(left, packed[:, 0:base]).astype(BF16)
            term[b, at, base : z.wide] = (dot_nn(left, packed[:, base:]) + dot_nn(left_out, placed)).astype(BF16)
            return carry

        lax.fori_loop(0, z.width // step, one, 0)
        away = pl.ds(pl.multiple_of((1 - core) * z.core_rows, 16), z.core_rows)
        send(term.at[b, away], term_in.at[b], w_s.at[b, 0], w_r.at[b, 0], (dp, s + 1 - 2 * core, t))

    def weights_y(b):
        wait(term_in.at[b], w_r.at[b, 0])
        here = pl.ds(pl.multiple_of(core * z.core_rows, 16), z.core_rows)
        yb[b] = (term[b, here].astype(F32) + term_in[b].astype(F32)).astype(BF16)
        for k in range(z.ny - 1):
            to = (dp + k + 1) % z.ny
            src = yb.at[b, pl.ds(pl.multiple_of(to * z.y_rows, 16), z.y_rows)]
            send(src, yr.at[b, k], w_s.at[b, 1], w_r.at[b, 1], (to, s, t))

    def weights_z(b):
        wait(yr.at[b], w_r.at[b, 1])
        total = yb[b, pl.ds(pl.multiple_of(dp * z.y_rows, 16), z.y_rows)].astype(F32)
        for k in range(z.ny - 1):
            total += yr[b, k].astype(F32)
        zw[b] = dot_nn(pad_ref[...], total.astype(BF16)).astype(BF16)

        def block(i):
            return pl.ds(pl.multiple_of(i * z.rp, 16), z.rp)

        pltpu.make_async_copy(zw.at[b, block(zl)], zr.at[b, zl], w_r.at[b, 2]).start()
        for k in range(z.nzl - 1):
            to = (zl + k + 1) % z.nzl
            send(zw.at[b, block(to)], zr.at[b, zl], w_s.at[b, 2], w_r.at[b, 2], (dp, 2 * to + core, t))

    def weights_end(b, w_out):
        wait(zr.at[b], w_r.at[b, 2])
        total = zr[b, 0].astype(F32)
        for k in range(1, z.nzl):
            total += zr[b, k].astype(F32)
        w_out[...] = total

    project(x_ref[...], ws_ref, qkv_s)
    attend(qkv_s, prob_s, mix_s, None)
    partial_and_send(0, lambda lanes: dot_nn(mix_s[...], wos_ref[:, lanes]))

    def add_input(lanes):
        return x_ref[:, lanes].astype(F32) * jnp.where(zh == 0, 1.0, 0.0)

    switch(0, add_input)

    wait(got.at[:, tile_lanes(xi, 0, z.reg)], go_r.at[0])
    wait(ge, go_r.at[1])
    for k in range(z.nx - 1):
        lanes = tile_lanes(xi, 0, z.reg)
        send(got.at[:, lanes], got.at[:, lanes], gag_s.at[0], gag_r.at[0, k], at_x(k))
        send(ge, geg.at[k], gag_s.at[1], gag_r.at[1, k], at_x(k))
    transposed(x_ref, lt_x)

    sum_z(0, ti, tie, tig)

    place_last(got, ge, xi)
    for k in range(z.nx - 1):
        who = (xi - k - 1 + z.nx) % z.nx
        wait(got.at[:, tile_lanes(who, 0, z.reg)], gag_r.at[0, k])
        wait(geg.at[k], gag_r.at[1, k])
        place_last(got, geg.at[k], who)
    gm_t[...] = dot_nt(got[...], wot_ref[...]).astype(BF16)
    transposed(got, lt_go)
    gather_x(0, ti, tie, tig)

    rows_i = lax.broadcasted_iota(jnp.int32, (n, n), 0)
    cols_i = lax.broadcasted_iota(jnp.int32, (n, n), 1)
    same = (rows_i & (ROWS - 1)) == (cols_i & (ROWS - 1))
    project(ti[...], wt_ref, qkv_t)
    attend(qkv_t, prob_t, mix_t, same)
    attend_back(qkv_t, prob_t, gm_t[...], grads.at[0])

    def back(b, weight_ref):
        def product(lanes):
            total = dot_nn(grads[b, 0], weight_ref[0:cols, lanes])
            for part in range(1, 3):
                total += dot_nn(grads[b, part], weight_ref[part * cols : (part + 1) * cols, lanes])
            return total

        return product

    partial_and_send(1, back(0, wt_ref))
    transposed(ti, lt_ti)
    weight_terms(0, lt_ti, lt_go, mix_t)
    switch(1)
    weights_y(0)
    sum_z(1, tg, tge, tgg, go_ref)
    weights_z(0)
    gather_x(1, tg, tge, tgg)

    grad_mixed_s = dot_nt(tg[...], wos_ref[...]).astype(BF16)
    attend_back(qkv_s, prob_s, grad_mixed_s, grads.at[1])
    partial_and_send(2, back(1, ws_ref))
    transposed(tg, lt_tg)
    weight_terms(1, lt_x, lt_tg, mix_s)

    def exchange(j):
        sum_x(2, j)
        send(sb.at[2, j], eb.at[j], eb_s.at[j], eb_r.at[j], (dp, s, (1 - zh) * z.nx + xi))

    def finish(j, k_sem):
        wait(eb.at[j], eb_r.at[j])
        lanes = tile_lanes(xi, j) if j < z.reg else last
        total = tg[:, lanes].astype(F32) + (sb[2, j].astype(F32) + eb[j].astype(F32))
        out_ref[:, lanes] = total.astype(BF16)
        for k in range(z.nx - 1):
            send(out_ref.at[:, lanes], out_ref.at[:, lanes], ag_s.at[2, j], ag_r.at[2, j, k_sem(k)], at_x(k))

    for j in range(z.reg):
        exchange(j)

    @pl.when(is_owner)
    def _():
        exchange(z.reg)

    weights_y(1)
    for j in range(z.reg):
        finish(j, lambda k: k)

    @pl.when(is_owner)
    def _():
        finish(z.reg, lambda k: 0)

    weights_z(1)
    weights_end(0, wt_out)
    for k in range(z.nx - 1):
        who = (xi - k - 1 + z.nx) % z.nx
        for j in range(z.reg):
            wait(out_ref.at[:, tile_lanes(who, j)], ag_r.at[2, j, k])

    @pl.when(jnp.logical_not(is_owner))
    def _():
        wait(out_ref.at[:, last], ag_r.at[2, z.reg, 0])

    weights_end(1, ws_out)

    for p in range(3):
        for j in range(z.reg):
            wait(rx.at[p, j], rx_s.at[p, j])
            wait(rx.at[p, j], ag_s.at[p, j])

        @pl.when(jnp.logical_not(is_owner))
        def _():
            wait(rx.at[p, z.reg, 0], rx_s.at[p, z.reg])

    sent = (2 * z.ns - 1) * ROWS
    for p in range(2):
        for j in range(z.reg):
            wait(zb.at[p, j, pl.ds(0, sent)], zb_s.at[p, j])
        wait(tig if p == 0 else tgg, ag_s.at[p, z.reg])

        @pl.when(is_owner)
        def _():
            wait(zb.at[p, 0, pl.ds(0, sent)], zb_s.at[p, z.reg])

    for j in range(z.reg):
        wait(eb.at[j], eb_s.at[j])

    @pl.when(is_owner)
    def _():
        wait(eb.at[z.reg], eb_s.at[z.reg])
        wait(rx.at[2, z.reg], ag_s.at[2, z.reg])
        wait(got.at[pl.ds(0, (z.ns - 1) * ROWS), last], go_s.at[1])

    wait(got.at[pl.ds(0, (z.ns - 1) * ROWS), pl.ds(0, z.reg * LANES)], go_s.at[0])
    wait(got.at[:, pl.ds(0, (z.nx - 1) * z.reg * LANES)], gag_s.at[0])
    wait(geg, gag_s.at[1])
    for b in range(2):
        wait(term_in.at[b], w_s.at[b, 0])
        wait(yr.at[b], w_s.at[b, 1])
        wait(zr.at[b, pl.ds(0, z.nzl - 1)], w_s.at[b, 2])


def run(z, *arrays):
    n, width, cols = z.tokens, z.width, z.cols
    chunks = z.reg + 1
    dma = pltpu.SemaphoreType.DMA
    vmem = pltpu.VMEM
    shared = z.per * ROWS
    return pl.pallas_call(
        functools.partial(kernel, z),
        out_shape=(
            jax.ShapeDtypeStruct((n, width), BF16),
            jax.ShapeDtypeStruct((z.rp, z.wide), F32),
            jax.ShapeDtypeStruct((z.rp, z.wide), F32),
        ),
        in_specs=[pl.BlockSpec(memory_space=pltpu.VMEM)] * len(arrays),
        out_specs=[pl.BlockSpec(memory_space=pltpu.VMEM)] * 3,
        scratch_shapes=[
            vmem((3, n, cols), BF16), vmem((3, n, cols), BF16),
            vmem((2, n, n), F32), vmem((2, n, n), F32),
            vmem((n, cols), BF16), vmem((n, cols), BF16), vmem((n, cols), BF16),
            vmem((2, 3, n, cols), BF16),
            vmem((3, n, width), BF16),
            vmem((3, chunks, z.nx - 1, n, LANES), BF16),
            vmem((3, chunks, n, LANES), BF16),
            vmem((2, z.reg, 2 * n, LANES), BF16),
            vmem((2, 2 * shared, LANES), BF16),
            vmem((chunks, n, LANES), BF16),
            vmem((n, width), BF16), vmem((shared, LANES), BF16), vmem((z.nx - 1, shared, LANES), BF16),
            vmem((n, width), BF16), vmem((shared, LANES), BF16), vmem((z.nx - 1, shared, LANES), BF16),
            vmem((n, width), BF16), vmem((shared, LANES), BF16), vmem((z.nx - 1, shared, LANES), BF16),
            vmem((width, n), BF16), vmem((width, n), BF16), vmem((width, n), BF16), vmem((width, n), BF16),
            vmem((2, width, z.wide), BF16), vmem((2, z.core_rows, z.wide), BF16),
            vmem((2, z.core_rows, z.wide), BF16), vmem((2, z.ny - 1, z.y_rows, z.wide), BF16),
            vmem((2, z.nzl * z.rp, z.wide), BF16), vmem((2, z.nzl, z.rp, z.wide), BF16),
            dma((3, chunks)), dma((3, chunks)),
            dma((2, chunks)), dma((2, chunks)),
            dma((3, chunks)), dma((3, chunks, z.nx - 1)),
            dma((2,)), dma((2,)), dma((2,)), dma((2, z.nx - 1)),
            dma((chunks,)), dma((chunks,)),
            dma((2, 3)), dma((2, 3)),
        ],
        compiler_params=pltpu.CompilerParams(
            collective_id=0, has_side_effects=True, vmem_limit_bytes=56 * 1024 * 1024
        ),
    )(*arrays)


def solution(mesh):
    def on_device(spatial_input, out_grad, qkv_spatial, out_spatial, qkv_temporal, out_temporal):
        width = spatial_input.shape[-1]
        tokens = spatial_input.shape[-2]
        z = Sizes(mesh.shape, tokens, width)
        cols = z.cols

        def flat(weight):
            return weight.transpose(1, 2, 0).reshape(3 * cols, width)

        grad, wt, ws = run(
            z,
            spatial_input.reshape(tokens, width), out_grad.reshape(tokens, width),
            flat(qkv_spatial), out_spatial, flat(qkv_temporal), out_temporal,
            row_order(z), row_pad(z),
        )

        def parts(w):
            return (
                w[: z.rr, : 3 * cols].reshape(z.rr, 3, cols),
                w[: z.rr, 3 * cols : 4 * cols].T,
            )

        qkv_t_grad, out_t_grad = parts(wt)
        qkv_s_grad, out_s_grad = parts(ws)
        return grad.reshape(spatial_input.shape), qkv_s_grad, out_s_grad, qkv_t_grad, out_t_grad

    placed = (
        P("dp", "sp", None, None),
        P("dp", "sp", None, None),
        P(None, None, "tp"),
        P("tp", None),
        P(None, None, "tp"),
        P("tp", None),
    )
    return jax.shard_map(
        on_device,
        mesh=mesh,
        in_specs=placed,
        out_specs=(
            P("dp", "sp", None, None),
            P(("sp", "dp"), None, "tp"),
            P("tp", ("sp", "dp")),
            P(("sp", "dp"), None, "tp"),
            P("tp", ("sp", "dp")),
        ),
        check_vma=False,
    )
```

time: 1140 us -> 127 us (0.11)
  the two profiles are of different devices: /device:TPU:6 before, /device:TPU:8 now
where the time goes in v1:
time: 127 us
  Pallas kernels  120 us (94%)
  local copies, waits for them, and re-layouts  6.45 us (5%)
    pallas_call x1, Pallas kernels, run(): pl.pallas_call(functools.partial(kernel, z), out_shape=(jax.ShapeDtypeStr...  120 us

profile of v1, /device:TPU:8, one launch (start us, length us, event | category | flops | bytes accessed | tf_op | source)
XLA Modules:
  0.0 126.7 jit_solution(11848485924430616378)
XLA Ops:
  0.6 119.6 %shard_map.119 = (bf16[256,1152]{1,0:T(8,128)(2,1)}, f32[32,640]{1,0:T(8,128)}, f32[32,640]{1,0:T(8,128)}) custom-call(bf16[256,1152]{1,0:T(8,128)(2,1)} %bitcast.15, bf16[256,1152]{1,0:T(8,128)(2,1)} %bitcast.16, bf16[432,1152]{1,0:T(8,128)(2,1)} %bitcast.13, bf16[144,1152]{1,0:T(8,128)(2,1)} %wos_ref.1, bf16[432,1152]{1,0:T(8,128)(2,1)} %bitcast.14, ...), custom_call_target="tpu_custom_call" | custom-call | tf_op jit(solution)/shard_map/pallas_call | solution.py:483
  120.3 0.8 slice.12
  121.1 1.5 %slice_bitcast_fusion = (f32[144,18]{0,1:T(8,128)}, f32[144,18]{0,1:T(8,128)}) fusion(f32[32,640]{1,0:T(8,128)} %get-tuple-element.10, f32[32,640]{1,0:T(8,128)} %get-tuple-element.9), kind=kLoop, calls=%fused_computation | loop fusion | bytes 41472 | tf_op jit(solution)/shard_map/transpose | solution.py:543
  122.5 0.8 slice.14
  123.3 0.7 reshape.37
  124.1 0.7 reshape.36
  124.8 1.9 %copy.14 = bf16[1,1,256,1152]{3,2,1,0:T(8,128)(2,1)} copy(bf16[1,1,256,1152]{3,2,1,0:T(8,128)(2,1)} %bitcast.17) | data formatting | bytes 1179648

commit v2 on v1

--- a/solution.py
+++ b/solution.py
@@ -42,7 +42,7 @@
         self.core_rows = width // 2
         self.y_rows = self.core_rows // self.ny
         self.rr = width // (self.ns * self.ny)
-        self.rp = -(-self.rr // 16) * 16
+        self.packed = -(-(self.wide // LANES) * self.rr // 16) * 16
 
 
 def row_order(z):
@@ -52,18 +52,21 @@
     return onehot.astype(jnp.bfloat16)
 
 
-def row_pad(z):
-    onehot = np.zeros((z.nzl * z.rp, z.y_rows), np.float32)
+def row_pack(z):
+    tiles = z.wide // LANES
+    onehot = np.zeros((z.nzl, z.packed, tiles, z.nzl, z.rr), np.float32)
     for chip in range(z.nzl):
-        for row in range(z.rr):
-            onehot[chip * z.rp + row, chip * z.rr + row] = 1.0
-    return onehot.astype(jnp.bfloat16)
+        for tile in range(tiles):
+            for row in range(z.rr):
+                onehot[chip, tile * z.rr + row, tile, chip, row] = 1.0
+    return onehot.reshape(z.nzl * z.packed, tiles * z.y_rows).astype(jnp.bfloat16)
 
 
 def kernel(
     z,
-    x_ref, go_ref, ws_ref, wos_ref, wt_ref, wot_ref, order_ref, pad_ref,
+    x_ref, ws_ref, wos_ref, go_hbm, wt_hbm, wot_hbm, order_hbm, pack_hbm,
     out_ref, wt_out, ws_out,
+    go_ref, wt_ref, wot_ref, order_ref, pack_ref, load_sems,
     qkv_s, qkv_t, prob_s, prob_t, mix_s, mix_t, gm_t, grads,
     pb, rx, sb, zb, ze, eb,
     ti, tie, tig, tg, tge, tgg, got, ge, geg,
@@ -86,8 +89,10 @@
         return (dp, s, zh * z.nx + (xi + k + 1) % z.nx)
 
     def at_z(i):
-        place = (zh * z.ns + s + i) % (2 * z.ns)
-        return place % z.ns, (dp, place % z.ns, (place // z.ns) * z.nx + xi)
+        away, way = z.nzl - i // 4, 1 - 2 * ((i % 4) // 2)
+        chip = (zh * z.nzl + zl + way * away + 2 * z.nzl) % (2 * z.nzl)
+        to = (chip % z.nzl) * 2 + (core + i + 1) % 2
+        return to, (dp, to, (chip // z.nzl) * z.nx + xi)
 
     def send(src, dst, ssem, rsem, dev):
         pltpu.make_async_remote_copy(
@@ -102,6 +107,15 @@
 
     def rows_of(i, base=0):
         return pl.ds(pl.multiple_of(base + i * ROWS, ROWS), ROWS)
+
+    loads = (
+        (go_hbm, go_ref), (order_hbm, order_ref), (wt_hbm, wt_ref), (wot_hbm, wot_ref), (pack_hbm, pack_ref)
+    )
+    for i, (src, dst) in enumerate(loads):
+        pltpu.make_async_copy(src, dst, load_sems.at[i]).start()
+
+    def loaded(i):
+        wait(loads[i][1], load_sems.at[i])
 
     barrier = pltpu.get_barrier_semaphore()
     for k in range(z.nx - 1):
@@ -113,8 +127,7 @@
         pl.semaphore_signal(barrier, inc=1, device_id=at_z(i)[1], device_id_type=MESH)
         return carry
 
-    lax.fori_loop(1, 2 * z.ns, greet, 0)
-    pl.semaphore_wait(barrier, (z.nx - 1) + (z.ny - 1) + (2 * z.ns - 1))
+    lax.fori_loop(2, 2 * z.ns + 1, greet, 0)
 
     def send_go(i, carry):
         to = (s + i) % z.ns
@@ -130,15 +143,16 @@
         send(go_ref.at[rows_of(to), last], ge.at[rows_of(s // z.nx)], go_s.at[1], go_r.at[1], (dp, to, t))
         return carry
 
-    pltpu.make_async_copy(
-        go_ref.at[rows_of(s), tile_lanes(xi, 0, z.reg)], got.at[rows_of(s), tile_lanes(xi, 0, z.reg)], go_r.at[0]
-    ).start()
-    lax.fori_loop(1, z.ns, send_go, 0)
-
-    @pl.when(is_owner)
-    def _():
-        pltpu.make_async_copy(go_ref.at[rows_of(s), last], ge.at[rows_of(s // z.nx)], go_r.at[1]).start()
-        lax.fori_loop(1, z.ns, send_go_last, 0)
+    def switch_out_grad():
+        pltpu.make_async_copy(
+            go_ref.at[rows_of(s), tile_lanes(xi, 0, z.reg)], got.at[rows_of(s), tile_lanes(xi, 0, z.reg)], go_r.at[0]
+        ).start()
+        lax.fori_loop(1, z.ns, send_go, 0)
+
+        @pl.when(is_owner)
+        def _():
+            pltpu.make_async_copy(go_ref.at[rows_of(s), last], ge.at[rows_of(s // z.nx)], go_r.at[1]).start()
+            lax.fori_loop(1, z.ns, send_go_last, 0)
 
     first_head = lax.broadcasted_iota(jnp.int32, (n, cols), 1) < HEAD_DIM
 
@@ -238,7 +252,7 @@
             send(sb.at[p, j, rows_of(to)], dst, zb_s.at[p, j], zb_r.at[p, j], dev)
             return carry
 
-        lax.fori_loop(1, 2 * z.ns, one, 0)
+        lax.fori_loop(2, 2 * z.ns + 1, one, 0)
 
     def switch(p, extra=None):
         for j in range(z.reg):
@@ -320,10 +334,12 @@
         total = yb[b, pl.ds(pl.multiple_of(dp * z.y_rows, 16), z.y_rows)].astype(F32)
         for k in range(z.ny - 1):
             total += yr[b, k].astype(F32)
-        zw[b] = dot_nn(pad_ref[...], total.astype(BF16)).astype(BF16)
+        total = total.astype(BF16)
+        stacked = jnp.concatenate([total[:, i : i + LANES] for i in range(0, z.wide, LANES)], axis=0)
+        zw[b] = dot_nn(pack_ref[...], stacked).astype(BF16)
 
         def block(i):
-            return pl.ds(pl.multiple_of(i * z.rp, 16), z.rp)
+            return pl.ds(pl.multiple_of(i * z.packed, 16), z.packed)
 
         pltpu.make_async_copy(zw.at[b, block(zl)], zr.at[b, zl], w_r.at[b, 2]).start()
         for k in range(z.nzl - 1):
@@ -339,7 +355,10 @@
 
     project(x_ref[...], ws_ref, qkv_s)
     attend(qkv_s, prob_s, mix_s, None)
+    pl.semaphore_wait(barrier, (z.nx - 1) + (z.ny - 1) + (2 * z.ns - 1))
     partial_and_send(0, lambda lanes: dot_nn(mix_s[...], wos_ref[:, lanes]))
+    loaded(0)
+    switch_out_grad()
 
     def add_input(lanes):
         return x_ref[:, lanes].astype(F32) * jnp.where(zh == 0, 1.0, 0.0)
@@ -352,6 +371,7 @@
         lanes = tile_lanes(xi, 0, z.reg)
         send(got.at[:, lanes], got.at[:, lanes], gag_s.at[0], gag_r.at[0, k], at_x(k))
         send(ge, geg.at[k], gag_s.at[1], gag_r.at[1, k], at_x(k))
+    loaded(1)
     transposed(x_ref, lt_x)
 
     sum_z(0, ti, tie, tig)
@@ -362,6 +382,8 @@
         wait(got.at[:, tile_lanes(who, 0, z.reg)], gag_r.at[0, k])
         wait(geg.at[k], gag_r.at[1, k])
         place_last(got, geg.at[k], who)
+    loaded(2)
+    loaded(3)
     gm_t[...] = dot_nt(got[...], wot_ref[...]).astype(BF16)
     transposed(got, lt_go)
     gather_x(0, ti, tie, tig)
@@ -388,6 +410,7 @@
     switch(1)
     weights_y(0)
     sum_z(1, tg, tge, tgg, go_ref)
+    loaded(4)
     weights_z(0)
     gather_x(1, tg, tge, tgg)
 
@@ -417,6 +440,7 @@
         exchange(z.reg)
 
     weights_y(1)
+    weights_z(1)
     for j in range(z.reg):
         finish(j, lambda k: k)
 
@@ -424,7 +448,6 @@
     def _():
         finish(z.reg, lambda k: 0)
 
-    weights_z(1)
     weights_end(0, wt_out)
     for k in range(z.nx - 1):
         who = (xi - k - 1 + z.nx) % z.nx
@@ -472,6 +495,31 @@
         wait(term_in.at[b], w_s.at[b, 0])
         wait(yr.at[b], w_s.at[b, 1])
         wait(zr.at[b, pl.ds(0, z.nzl - 1)], w_s.at[b, 2])
+
+
+def finish_kernel(z, grad_ref, wt_ref, ws_ref, grad_out, qkv_s_out, out_s_out, qkv_t_out, out_t_out, sem):
+    copy = pltpu.make_async_copy(grad_ref, grad_out, sem)
+    copy.start()
+    for w_ref, qkv_out, out_out in ((ws_ref, qkv_s_out, out_s_out), (wt_ref, qkv_t_out, out_t_out)):
+        rows = [w_ref[i * z.rr : (i + 1) * z.rr, :] for i in range(z.wide // LANES)]
+        rows = jnp.concatenate(rows, axis=1)
+        for part in range(3):
+            qkv_out[:, part, :] = rows[:, part * z.cols : (part + 1) * z.cols]
+        out_out[...] = rows[:, 3 * z.cols : 4 * z.cols]
+    copy.wait()
+
+
+def finish(z, *arrays):
+    hbm, vmem = pl.BlockSpec(memory_space=pltpu.HBM), pl.BlockSpec(memory_space=pltpu.VMEM)
+    qkv = jax.ShapeDtypeStruct((z.rr, 3, z.cols), F32)
+    out = jax.ShapeDtypeStruct((z.rr, z.cols), F32)
+    return pl.pallas_call(
+        functools.partial(finish_kernel, z),
+        out_shape=(jax.ShapeDtypeStruct((z.tokens, z.width), BF16), qkv, out, qkv, out),
+        in_specs=[hbm, vmem, vmem],
+        out_specs=[hbm] + [vmem] * 4,
+        scratch_shapes=[pltpu.SemaphoreType.DMA],
+    )(*arrays)
 
 
 def run(z, *arrays):
@@ -484,12 +532,14 @@
         functools.partial(kernel, z),
         out_shape=(
             jax.ShapeDtypeStruct((n, width), BF16),
-            jax.ShapeDtypeStruct((z.rp, z.wide), F32),
-            jax.ShapeDtypeStruct((z.rp, z.wide), F32),
+            jax.ShapeDtypeStruct((z.packed, LANES), F32),
+            jax.ShapeDtypeStruct((z.packed, LANES), F32),
         ),
-        in_specs=[pl.BlockSpec(memory_space=pltpu.VMEM)] * len(arrays),
+        in_specs=[pl.BlockSpec(memory_space=pltpu.VMEM)] * 3 + [pl.BlockSpec(memory_space=pl.ANY)] * 5,
         out_specs=[pl.BlockSpec(memory_space=pltpu.VMEM)] * 3,
         scratch_shapes=[
+            vmem((n, width), BF16), vmem((3 * cols, width), BF16), vmem((cols, width), BF16),
+            vmem((width, width), BF16), vmem((z.nzl * z.packed, z.wide // LANES * z.y_rows), BF16), dma((5,)),
             vmem((3, n, cols), BF16), vmem((3, n, cols), BF16),
             vmem((2, n, n), F32), vmem((2, n, n), F32),
             vmem((n, cols), BF16), vmem((n, cols), BF16), vmem((n, cols), BF16),
@@ -506,7 +556,7 @@
             vmem((width, n), BF16), vmem((width, n), BF16), vmem((width, n), BF16), vmem((width, n), BF16),
             vmem((2, width, z.wide), BF16), vmem((2, z.core_rows, z.wide), BF16),
             vmem((2, z.core_rows, z.wide), BF16), vmem((2, z.ny - 1, z.y_rows, z.wide), BF16),
-            vmem((2, z.nzl * z.rp, z.wide), BF16), vmem((2, z.nzl, z.rp, z.wide), BF16),
+            vmem((2, z.nzl * z.packed, LANES), BF16), vmem((2, z.nzl, z.packed, LANES), BF16),
             dma((3, chunks)), dma((3, chunks)),
             dma((2, chunks)), dma((2, chunks)),
             dma((3, chunks)), dma((3, chunks, z.nx - 1)),
@@ -532,20 +582,12 @@
 
         grad, wt, ws = run(
             z,
-            spatial_input.reshape(tokens, width), out_grad.reshape(tokens, width),
-            flat(qkv_spatial), out_spatial, flat(qkv_temporal), out_temporal,
-            row_order(z), row_pad(z),
+            spatial_input.reshape(tokens, width), flat(qkv_spatial), out_spatial,
+            out_grad.reshape(tokens, width), flat(qkv_temporal), out_temporal,
+            row_order(z), row_pack(z),
         )
-
-        def parts(w):
-            return (
-                w[: z.rr, : 3 * cols].reshape(z.rr, 3, cols),
-                w[: z.rr, 3 * cols : 4 * cols].T,
-            )
-
-        qkv_t_grad, out_t_grad = parts(wt)
-        qkv_s_grad, out_s_grad = parts(ws)
-        return grad.reshape(spatial_input.shape), qkv_s_grad, out_s_grad, qkv_t_grad, out_t_grad
+        grad, qkv_s_grad, out_s_grad, qkv_t_grad, out_t_grad = finish(z, grad, wt, ws)
+        return grad.reshape(spatial_input.shape), qkv_s_grad, out_s_grad.T, qkv_t_grad, out_t_grad.T
 
     placed = (
         P("dp", "sp", None, None),

time: 127 us -> 133 us (1.047)
  the two profiles are of different devices: /device:TPU:8 before, /device:TPU:6 now
where the time goes in v2:
time: 133 us; the launch traced here: 131 us
  Pallas kernels  131 us (98%)
    pallas_call x1, Pallas kernels, run(): pl.pallas_call(functools.partial(kernel, z), out_shape=(jax.ShapeDtypeStr...  110 us
    pallas_call x1, Pallas kernels, finish(): pl.pallas_call(functools.partial(finish_kernel, z), out_shape=(jax.ShapeD...  20.5 us

profile of v2, /device:TPU:6, one launch (start us, length us, event | category | flops | bytes accessed | tf_op | source)
XLA Modules:
  0.0 131.3 jit_solution(1408058075982044416)
XLA Ops:
  0.6 110.2 %shard_map.119 = (bf16[256,1152]{1,0:T(8,128)(2,1)}, f32[96,128]{1,0:T(8,128)}, f32[96,128]{1,0:T(8,128)}) custom-call(bf16[256,1152]{1,0:T(8,128)(2,1)} %bitcast.13, bf16[432,1152]{1,0:T(8,128)(2,1)} %bitcast.11, bf16[144,1152]{1,0:T(8,128)(2,1)} %wos_ref.1, bf16[256,1152]{1,0:T(8,128)(2,1)} %bitcast.14, bf16[432,1152]{1,0:T(8,128)(2,1)} %bitcast.12, ...), custom_call_target="tpu_custom_call" | custom-call | tf_op jit(solution)/shard_map/pallas_call | solution.py:531
  110.8 20.5 %shard_map.120 = (bf16[256,1152]{1,0:T(8,128)(2,1)}, f32[18,3,144]{2,1,0:T(4,128)}, f32[18,144]{1,0:T(8,128)}, f32[18,3,144]{2,1,0:T(4,128)}, f32[18,144]{1,0:T(8,128)}) custom-call(bf16[256,1152]{1,0:T(8,128)(2,1)} %get-tuple-element.13.grad_ref, f32[96,128]{1,0:T(8,128)} %get-tuple-element.14.wt_ref, f32[96,128]{1,0:T(8,128)} %get-tuple-element.15.ws_ref), custom_call_target="tpu_custom_call" | custom-call | tf_op jit(solution)/shard_map/pallas_call | solution.py:516

commit v3 on v2

--- a/solution.py
+++ b/solution.py
@@ -64,15 +64,15 @@
 
 def kernel(
     z,
-    x_ref, ws_ref, wos_ref, go_hbm, wt_hbm, wot_hbm, order_hbm, pack_hbm,
+    x_hbm, ws_hbm, wos_hbm, go_hbm, wt_hbm, wot_hbm, order_hbm, pack_hbm,
     out_ref, wt_out, ws_out,
-    go_ref, wt_ref, wot_ref, order_ref, pack_ref, load_sems,
-    qkv_s, qkv_t, prob_s, prob_t, mix_s, mix_t, gm_t, grads,
+    x_ref, ws_ref, wos_ref, go_ref, wt_ref, wot_ref, order_ref, pack_ref, load_sems,
+    qkv_s, qkv_t, prob_s, prob_t, mix_s, mix_t, mix_ts, gm_s, gm_t, grads,
     pb, rx, sb, zb, ze, eb,
-    ti, tie, tig, tg, tge, tgg, got, ge, geg,
+    ti, tie, tig, tg, tge, tgg,
     lt_x, lt_ti, lt_go, lt_tg,
     term, term_in, yb, yr, zw, zr,
-    rx_s, rx_r, zb_s, zb_r, ag_s, ag_r, go_s, go_r, gag_s, gag_r, eb_s, eb_r,
+    rx_s, rx_r, zb_s, zb_r, ag_s, ag_r, hd_s, hd_r, eb_s, eb_r,
     w_s, w_r,
 ):
     n = z.tokens
@@ -102,57 +102,59 @@
     def wait(ref, sem):
         pltpu.make_async_copy(ref, ref, sem).wait()
 
+    leaving = []
+
+    def on_leaving():
+        for ref, place, sem, sem_place, of_owner in leaving:
+            def gone():
+                wait(ref.at[place] if place else ref, sem.at[sem_place])
+
+            if of_owner is None:
+                gone()
+            else:
+                pl.when(is_owner if of_owner else jnp.logical_not(is_owner))(gone)
+
+    sent_z = pl.ds(0, (2 * z.ns - 1) * ROWS)
+    sent_sp = pl.ds(0, (z.ns - 1) * ROWS)
+
     def tile_lanes(who, j, count=1):
         return pl.ds(pl.multiple_of((who * z.reg + j) * LANES, LANES), count * LANES)
 
     def rows_of(i, base=0):
         return pl.ds(pl.multiple_of(base + i * ROWS, ROWS), ROWS)
 
-    loads = (
-        (go_hbm, go_ref), (order_hbm, order_ref), (wt_hbm, wt_ref), (wot_hbm, wot_ref), (pack_hbm, pack_ref)
-    )
-    for i, (src, dst) in enumerate(loads):
-        pltpu.make_async_copy(src, dst, load_sems.at[i]).start()
-
-    def loaded(i):
-        wait(loads[i][1], load_sems.at[i])
-
     barrier = pltpu.get_barrier_semaphore()
+    def greet(i, carry):
+        pl.semaphore_signal(barrier, inc=1, device_id=at_z(i)[1], device_id_type=MESH)
+        return carry
+
+    lax.fori_loop(2, 2 * z.ns + 1, greet, 0)
     for k in range(z.nx - 1):
         pl.semaphore_signal(barrier, inc=1, device_id=at_x(k), device_id_type=MESH)
     for k in range(z.ny - 1):
         pl.semaphore_signal(barrier, inc=1, device_id=((dp + k + 1) % z.ny, s, t), device_id_type=MESH)
 
-    def greet(i, carry):
-        pl.semaphore_signal(barrier, inc=1, device_id=at_z(i)[1], device_id_type=MESH)
-        return carry
-
-    lax.fori_loop(2, 2 * z.ns + 1, greet, 0)
-
-    def send_go(i, carry):
-        to = (s + i) % z.ns
-        send(
-            go_ref.at[rows_of(to), tile_lanes(xi, 0, z.reg)],
-            got.at[rows_of(s), tile_lanes(xi, 0, z.reg)],
-            go_s.at[0], go_r.at[0], (dp, to, t),
-        )
-        return carry
-
-    def send_go_last(i, carry):
-        to = (s + i) % z.ns
-        send(go_ref.at[rows_of(to), last], ge.at[rows_of(s // z.nx)], go_s.at[1], go_r.at[1], (dp, to, t))
-        return carry
-
-    def switch_out_grad():
-        pltpu.make_async_copy(
-            go_ref.at[rows_of(s), tile_lanes(xi, 0, z.reg)], got.at[rows_of(s), tile_lanes(xi, 0, z.reg)], go_r.at[0]
-        ).start()
-        lax.fori_loop(1, z.ns, send_go, 0)
-
-        @pl.when(is_owner)
-        def _():
-            pltpu.make_async_copy(go_ref.at[rows_of(s), last], ge.at[rows_of(s // z.nx)], go_r.at[1]).start()
-            lax.fori_loop(1, z.ns, send_go_last, 0)
+    loads = (
+        (x_hbm, x_ref), (ws_hbm, ws_ref), (wos_hbm, wos_ref), (wot_hbm, wot_ref), (go_hbm, go_ref),
+        (order_hbm, order_ref), (wt_hbm, wt_ref), (pack_hbm, pack_ref),
+    )
+    for i, (src, dst) in enumerate(loads):
+        pltpu.make_async_copy(src, dst, load_sems.at[i]).start()
+
+    def loaded(*which):
+        for i in which:
+            wait(loads[i][1], load_sems.at[i])
+
+    def switch_heads(b, src, dst):
+        pltpu.make_async_copy(src.at[rows_of(s)], dst.at[rows_of(s)], hd_r.at[b]).start()
+
+        def one(i, carry):
+            to = (s + i) % z.ns
+            send(src.at[rows_of(to)], dst.at[rows_of(s)], hd_s.at[b], hd_r.at[b], (dp, to, t))
+            return carry
+
+        lax.fori_loop(1, z.ns, one, 0)
+        leaving.append((dst, (sent_sp,), hd_s, (b,), None))
 
     first_head = lax.broadcasted_iota(jnp.int32, (n, cols), 1) < HEAD_DIM
 
@@ -208,8 +210,11 @@
         for k in range(z.nx - 1):
             to = (xi + k + 1) % z.nx
             send(pb.at[p, :, tile_lanes(to, j)], rx.at[p, j, k], rx_s.at[p, j], rx_r.at[p, j], at_x(k))
+        leaving.append((rx, (p, j,), rx_s, (p, j,), None))
 
     def send_x_last(p):
+        leaving.append((rx, (p, z.reg, 0,), rx_s, (p, z.reg,), False))
+
         @pl.when(jnp.logical_not(is_owner))
         def _():
             k = (owner - xi - 1 + z.nx) % z.nx
@@ -253,6 +258,7 @@
             return carry
 
         lax.fori_loop(2, 2 * z.ns + 1, one, 0)
+        leaving.append((zb, (p, 0, sent_z,), zb_s, (p, j,), None if j < z.reg else True))
 
     def switch(p, extra=None):
         for j in range(z.reg):
@@ -274,6 +280,7 @@
             full[:, lanes] = total.astype(BF16)
             for k in range(z.nx - 1):
                 send(full.at[:, lanes], full.at[:, lanes], ag_s.at[p, j], ag_r.at[p, j, k], at_x(k))
+            leaving.append((rx, (p, j,), ag_s, (p, j,), None))
         wait(ze.at[p], zb_r.at[p, z.reg])
         half = z.per * ROWS
         for i in range(z.per):
@@ -284,6 +291,7 @@
             mine[i * ROWS : (i + 1) * ROWS, :] = total.astype(BF16)
         for k in range(z.nx - 1):
             send(mine, others.at[k], ag_s.at[p, z.reg], ag_r.at[p, z.reg, k], at_x(k))
+        leaving.append((others, (), ag_s, (p, z.reg,), None))
 
     def place_last(full, block, who):
         for i in range(z.per):
@@ -319,6 +327,7 @@
         lax.fori_loop(0, z.width // step, one, 0)
         away = pl.ds(pl.multiple_of((1 - core) * z.core_rows, 16), z.core_rows)
         send(term.at[b, away], term_in.at[b], w_s.at[b, 0], w_r.at[b, 0], (dp, s + 1 - 2 * core, t))
+        leaving.append((term_in, (b,), w_s, (b, 0,), None))
 
     def weights_y(b):
         wait(term_in.at[b], w_r.at[b, 0])
@@ -328,6 +337,7 @@
             to = (dp + k + 1) % z.ny
             src = yb.at[b, pl.ds(pl.multiple_of(to * z.y_rows, 16), z.y_rows)]
             send(src, yr.at[b, k], w_s.at[b, 1], w_r.at[b, 1], (to, s, t))
+        leaving.append((yr, (b,), w_s, (b, 1,), None))
 
     def weights_z(b):
         wait(yr.at[b], w_r.at[b, 1])
@@ -345,6 +355,7 @@
         for k in range(z.nzl - 1):
             to = (zl + k + 1) % z.nzl
             send(zw.at[b, block(to)], zr.at[b, zl], w_s.at[b, 2], w_r.at[b, 2], (dp, 2 * to + core, t))
+        leaving.append((zr, (b, pl.ds(0, z.nzl - 1),), w_s, (b, 2,), None))
 
     def weights_end(b, w_out):
         wait(zr.at[b], w_r.at[b, 2])
@@ -353,39 +364,25 @@
             total += zr[b, k].astype(F32)
         w_out[...] = total
 
+    loaded(0, 1)
     project(x_ref[...], ws_ref, qkv_s)
     attend(qkv_s, prob_s, mix_s, None)
+    loaded(2)
     pl.semaphore_wait(barrier, (z.nx - 1) + (z.ny - 1) + (2 * z.ns - 1))
     partial_and_send(0, lambda lanes: dot_nn(mix_s[...], wos_ref[:, lanes]))
-    loaded(0)
-    switch_out_grad()
+    loaded(3, 4)
+    gm_s[...] = dot_nt(go_ref[...], wot_ref[...]).astype(BF16)
 
     def add_input(lanes):
         return x_ref[:, lanes].astype(F32) * jnp.where(zh == 0, 1.0, 0.0)
 
     switch(0, add_input)
-
-    wait(got.at[:, tile_lanes(xi, 0, z.reg)], go_r.at[0])
-    wait(ge, go_r.at[1])
-    for k in range(z.nx - 1):
-        lanes = tile_lanes(xi, 0, z.reg)
-        send(got.at[:, lanes], got.at[:, lanes], gag_s.at[0], gag_r.at[0, k], at_x(k))
-        send(ge, geg.at[k], gag_s.at[1], gag_r.at[1, k], at_x(k))
-    loaded(1)
+    switch_heads(0, gm_s, gm_t)
+    loaded(5)
     transposed(x_ref, lt_x)
-
+    transposed(go_ref, lt_go)
     sum_z(0, ti, tie, tig)
-
-    place_last(got, ge, xi)
-    for k in range(z.nx - 1):
-        who = (xi - k - 1 + z.nx) % z.nx
-        wait(got.at[:, tile_lanes(who, 0, z.reg)], gag_r.at[0, k])
-        wait(geg.at[k], gag_r.at[1, k])
-        place_last(got, geg.at[k], who)
-    loaded(2)
-    loaded(3)
-    gm_t[...] = dot_nt(got[...], wot_ref[...]).astype(BF16)
-    transposed(got, lt_go)
+    loaded(6)
     gather_x(0, ti, tie, tig)
 
     rows_i = lax.broadcasted_iota(jnp.int32, (n, n), 0)
@@ -393,6 +390,8 @@
     same = (rows_i & (ROWS - 1)) == (cols_i & (ROWS - 1))
     project(ti[...], wt_ref, qkv_t)
     attend(qkv_t, prob_t, mix_t, same)
+    switch_heads(1, mix_t, mix_ts)
+    wait(gm_t, hd_r.at[0])
     attend_back(qkv_t, prob_t, gm_t[...], grads.at[0])
 
     def back(b, weight_ref):
@@ -406,11 +405,12 @@
 
     partial_and_send(1, back(0, wt_ref))
     transposed(ti, lt_ti)
-    weight_terms(0, lt_ti, lt_go, mix_t)
+    wait(mix_ts, hd_r.at[1])
+    weight_terms(0, lt_ti, lt_go, mix_ts)
     switch(1)
     weights_y(0)
     sum_z(1, tg, tge, tgg, go_ref)
-    loaded(4)
+    loaded(7)
     weights_z(0)
     gather_x(1, tg, tge, tgg)
 
@@ -423,6 +423,7 @@
     def exchange(j):
         sum_x(2, j)
         send(sb.at[2, j], eb.at[j], eb_s.at[j], eb_r.at[j], (dp, s, (1 - zh) * z.nx + xi))
+        leaving.append((eb, (j,), eb_s, (j,), None if j < z.reg else True))
 
     def finish(j, k_sem):
         wait(eb.at[j], eb_r.at[j])
@@ -431,6 +432,7 @@
         out_ref[:, lanes] = total.astype(BF16)
         for k in range(z.nx - 1):
             send(out_ref.at[:, lanes], out_ref.at[:, lanes], ag_s.at[2, j], ag_r.at[2, j, k_sem(k)], at_x(k))
+        leaving.append((rx, (2, j,), ag_s, (2, j,), None if j < z.reg else True))
 
     for j in range(z.reg):
         exchange(j)
@@ -460,65 +462,28 @@
 
     weights_end(1, ws_out)
 
-    for p in range(3):
-        for j in range(z.reg):
-            wait(rx.at[p, j], rx_s.at[p, j])
-            wait(rx.at[p, j], ag_s.at[p, j])
-
-        @pl.when(jnp.logical_not(is_owner))
-        def _():
-            wait(rx.at[p, z.reg, 0], rx_s.at[p, z.reg])
-
-    sent = (2 * z.ns - 1) * ROWS
-    for p in range(2):
-        for j in range(z.reg):
-            wait(zb.at[p, j, pl.ds(0, sent)], zb_s.at[p, j])
-        wait(tig if p == 0 else tgg, ag_s.at[p, z.reg])
-
-        @pl.when(is_owner)
-        def _():
-            wait(zb.at[p, 0, pl.ds(0, sent)], zb_s.at[p, z.reg])
-
-    for j in range(z.reg):
-        wait(eb.at[j], eb_s.at[j])
-
-    @pl.when(is_owner)
-    def _():
-        wait(eb.at[z.reg], eb_s.at[z.reg])
-        wait(rx.at[2, z.reg], ag_s.at[2, z.reg])
-        wait(got.at[pl.ds(0, (z.ns - 1) * ROWS), last], go_s.at[1])
-
-    wait(got.at[pl.ds(0, (z.ns - 1) * ROWS), pl.ds(0, z.reg * LANES)], go_s.at[0])
-    wait(got.at[:, pl.ds(0, (z.nx - 1) * z.reg * LANES)], gag_s.at[0])
-    wait(geg, gag_s.at[1])
-    for b in range(2):
-        wait(term_in.at[b], w_s.at[b, 0])
-        wait(yr.at[b], w_s.at[b, 1])
-        wait(zr.at[b, pl.ds(0, z.nzl - 1)], w_s.at[b, 2])
-
-
-def finish_kernel(z, grad_ref, wt_ref, ws_ref, grad_out, qkv_s_out, out_s_out, qkv_t_out, out_t_out, sem):
-    copy = pltpu.make_async_copy(grad_ref, grad_out, sem)
-    copy.start()
+    on_leaving()
+
+
+def finish_kernel(z, grad_ref, wt_ref, ws_ref, grad_out, qkv_s_out, out_s_out, qkv_t_out, out_t_out):
+    grad_out[...] = grad_ref[...]
     for w_ref, qkv_out, out_out in ((ws_ref, qkv_s_out, out_s_out), (wt_ref, qkv_t_out, out_t_out)):
         rows = [w_ref[i * z.rr : (i + 1) * z.rr, :] for i in range(z.wide // LANES)]
         rows = jnp.concatenate(rows, axis=1)
         for part in range(3):
             qkv_out[:, part, :] = rows[:, part * z.cols : (part + 1) * z.cols]
         out_out[...] = rows[:, 3 * z.cols : 4 * z.cols]
-    copy.wait()
 
 
 def finish(z, *arrays):
-    hbm, vmem = pl.BlockSpec(memory_space=pltpu.HBM), pl.BlockSpec(memory_space=pltpu.VMEM)
+    vmem = pl.BlockSpec(memory_space=pltpu.VMEM)
     qkv = jax.ShapeDtypeStruct((z.rr, 3, z.cols), F32)
     out = jax.ShapeDtypeStruct((z.rr, z.cols), F32)
     return pl.pallas_call(
         functools.partial(finish_kernel, z),
         out_shape=(jax.ShapeDtypeStruct((z.tokens, z.width), BF16), qkv, out, qkv, out),
-        in_specs=[hbm, vmem, vmem],
-        out_specs=[hbm] + [vmem] * 4,
-        scratch_shapes=[pltpu.SemaphoreType.DMA],
+        in_specs=[vmem] * 3,
+        out_specs=[vmem] * 5,
     )(*arrays)
 
 
@@ -535,14 +500,16 @@
             jax.ShapeDtypeStruct((z.packed, LANES), F32),
             jax.ShapeDtypeStruct((z.packed, LANES), F32),
         ),
-        in_specs=[pl.BlockSpec(memory_space=pltpu.VMEM)] * 3 + [pl.BlockSpec(memory_space=pl.ANY)] * 5,
+        in_specs=[pl.BlockSpec(memory_space=pl.ANY)] * len(arrays),
         out_specs=[pl.BlockSpec(memory_space=pltpu.VMEM)] * 3,
         scratch_shapes=[
             vmem((n, width), BF16), vmem((3 * cols, width), BF16), vmem((cols, width), BF16),
-            vmem((width, width), BF16), vmem((z.nzl * z.packed, z.wide // LANES * z.y_rows), BF16), dma((5,)),
+            vmem((n, width), BF16), vmem((3 * cols, width), BF16), vmem((cols, width), BF16),
+            vmem((width, width), BF16), vmem((z.nzl * z.packed, z.wide // LANES * z.y_rows), BF16), dma((8,)),
             vmem((3, n, cols), BF16), vmem((3, n, cols), BF16),
             vmem((2, n, n), F32), vmem((2, n, n), F32),
             vmem((n, cols), BF16), vmem((n, cols), BF16), vmem((n, cols), BF16),
+            vmem((n, cols), BF16), vmem((n, cols), BF16),
             vmem((2, 3, n, cols), BF16),
             vmem((3, n, width), BF16),
             vmem((3, chunks, z.nx - 1, n, LANES), BF16),
@@ -552,7 +519,6 @@
             vmem((chunks, n, LANES), BF16),
             vmem((n, width), BF16), vmem((shared, LANES), BF16), vmem((z.nx - 1, shared, LANES), BF16),
             vmem((n, width), BF16), vmem((shared, LANES), BF16), vmem((z.nx - 1, shared, LANES), BF16),
-            vmem((n, width), BF16), vmem((shared, LANES), BF16), vmem((z.nx - 1, shared, LANES), BF16),
             vmem((width, n), BF16), vmem((width, n), BF16), vmem((width, n), BF16), vmem((width, n), BF16),
             vmem((2, width, z.wide), BF16), vmem((2, z.core_rows, z.wide), BF16),
             vmem((2, z.core_rows, z.wide), BF16), vmem((2, z.ny - 1, z.y_rows, z.wide), BF16),
@@ -560,7 +526,7 @@
             dma((3, chunks)), dma((3, chunks)),
             dma((2, chunks)), dma((2, chunks)),
             dma((3, chunks)), dma((3, chunks, z.nx - 1)),
-            dma((2,)), dma((2,)), dma((2,)), dma((2, z.nx - 1)),
+            dma((2,)), dma((2,)),
             dma((chunks,)), dma((chunks,)),
             dma((2, 3)), dma((2, 3)),
         ],

time: 133 us -> 112 us (0.84)
  Pallas kernels: 131 us -> 110 us
    pallas_call x1, Pallas kernels: 20.5 us -> 2.07 us  [finish(): pl.pallas_call(functools.partial(finish_kernel, z), out_shape=(jax.ShapeD...]
    pallas_call x1, Pallas kernels: 110 us -> 108 us  [run(): pl.pallas_call(functools.partial(kernel, z), out_shape=(jax.ShapeDtypeStr...]
where the time goes in v3:
time: 112 us; the launch traced here: 111 us
  Pallas kernels  110 us (98%)
    pallas_call x1, Pallas kernels, run(): pl.pallas_call(functools.partial(kernel, z), out_shape=(jax.ShapeDtypeStr...  108 us

profile of v3, /device:TPU:6, one launch (start us, length us, event | category | flops | bytes accessed | tf_op | source)
XLA Modules:
  0.0 110.5 jit_solution(12308313452255510881)
XLA Ops:
  0.6 107.8 %shard_map.119 = (bf16[256,1152]{1,0:T(8,128)(2,1)}, f32[96,128]{1,0:T(8,128)}, f32[96,128]{1,0:T(8,128)}) custom-call(bf16[256,1152]{1,0:T(8,128)(2,1)} %bitcast.13, bf16[432,1152]{1,0:T(8,128)(2,1)} %bitcast.11, bf16[144,1152]{1,0:T(8,128)(2,1)} %wos_hbm.1, bf16[256,1152]{1,0:T(8,128)(2,1)} %bitcast.14, bf16[432,1152]{1,0:T(8,128)(2,1)} %bitcast.12, ...), custom_call_target="tpu_custom_call" | custom-call | tf_op jit(solution)/shard_map/pallas_call | solution.py:496
  108.5 2.1 %shard_map.120 = (bf16[256,1152]{1,0:T(8,128)(2,1)}, f32[18,3,144]{2,1,0:T(4,128)}, f32[18,144]{1,0:T(8,128)}, f32[18,3,144]{2,1,0:T(4,128)}, f32[18,144]{1,0:T(8,128)}) custom-call(bf16[256,1152]{1,0:T(8,128)(2,1)} %get-tuple-element.13.grad_ref, f32[96,128]{1,0:T(8,128)} %get-tuple-element.14.wt_ref, f32[96,128]{1,0:T(8,128)} %get-tuple-element.15.ws_ref), custom_call_target="tpu_custom_call" | custom-call | tf_op jit(solution)/shard_map/pallas_call | solution.py:482

commit v4 on v3

--- a/solution.py
+++ b/solution.py
@@ -68,7 +68,7 @@
     out_ref, wt_out, ws_out,
     x_ref, ws_ref, wos_ref, go_ref, wt_ref, wot_ref, order_ref, pack_ref, load_sems,
     qkv_s, qkv_t, prob_s, prob_t, mix_s, mix_t, mix_ts, gm_s, gm_t, grads,
-    pb, rx, sb, zb, ze, eb,
+    pb, pbl, rx, rxl, sb, sbl, zb, ze, spare, eb, ebl, oute, outg,
     ti, tie, tig, tg, tge, tgg,
     lt_x, lt_ti, lt_go, lt_tg,
     term, term_in, yb, yr, zw, zr,
@@ -81,8 +81,6 @@
     dp, s, t = lax.axis_index("dp"), lax.axis_index("sp"), lax.axis_index("tp")
     zh, xi = t // z.nx, t % z.nx
     zl, core = s // 2, s % 2
-    owner = s % z.nx
-    is_owner = xi == owner
     last = pl.ds((z.tiles - 1) * LANES, LANES)
 
     def at_x(k):
@@ -105,14 +103,8 @@
     leaving = []
 
     def on_leaving():
-        for ref, place, sem, sem_place, of_owner in leaving:
-            def gone():
-                wait(ref.at[place] if place else ref, sem.at[sem_place])
-
-            if of_owner is None:
-                gone()
-            else:
-                pl.when(is_owner if of_owner else jnp.logical_not(is_owner))(gone)
+        for ref, place, sem, sem_place in leaving:
+            wait(ref.at[place] if place else ref, sem.at[sem_place])
 
     sent_z = pl.ds(0, (2 * z.ns - 1) * ROWS)
     sent_sp = pl.ds(0, (z.ns - 1) * ROWS)
@@ -154,7 +146,7 @@
             return carry
 
         lax.fori_loop(1, z.ns, one, 0)
-        leaving.append((dst, (sent_sp,), hd_s, (b,), None))
+        leaving.append((dst, (sent_sp,), hd_s, (b,)))
 
     first_head = lax.broadcasted_iota(jnp.int32, (n, cols), 1) < HEAD_DIM
 
@@ -197,7 +189,7 @@
             grads_ref[part] = both_heads(pair).astype(BF16)
 
     def transposed(rows_ref, lt_ref):
-        step = 192 if z.width % 192 == 0 else 160
+        step = z.width // 2
 
         def one(i, carry):
             at = pl.ds(pl.multiple_of(i * step, 16), step)
@@ -210,18 +202,24 @@
         for k in range(z.nx - 1):
             to = (xi + k + 1) % z.nx
             send(pb.at[p, :, tile_lanes(to, j)], rx.at[p, j, k], rx_s.at[p, j], rx_r.at[p, j], at_x(k))
-        leaving.append((rx, (p, j,), rx_s, (p, j,), None))
+        leaving.append((rx, (p, j), rx_s, (p, j)))
+
+    share = z.per * ROWS
+
+    def class_of(x_place):
+        return (x_place - s + z.ns) % z.nx
+
+    def share_rows(x_place):
+        return pl.ds(pl.multiple_of(class_of(x_place) * share, ROWS), share)
+
+    def member(x_place, i):
+        return class_of(x_place) + z.nx * i
 
     def send_x_last(p):
-        leaving.append((rx, (p, z.reg, 0,), rx_s, (p, z.reg,), False))
-
-        @pl.when(jnp.logical_not(is_owner))
-        def _():
-            k = (owner - xi - 1 + z.nx) % z.nx
-            send(
-                pb.at[p, :, last], rx.at[p, z.reg, k], rx_s.at[p, z.reg], rx_r.at[p, z.reg],
-                (dp, s, zh * z.nx + owner),
-            )
+        for k in range(z.nx - 1):
+            to = (xi + k + 1) % z.nx
+            send(pbl.at[p, share_rows(to)], rxl.at[p, k], rx_s.at[p, z.reg], rx_r.at[p, z.reg], at_x(k))
+        leaving.append((rxl, (p,), rx_s, (p, z.reg)))
 
     def partial_and_send(p, product):
         for j in range(z.reg):
@@ -229,46 +227,66 @@
                 lanes = slice((who * z.reg + j) * LANES, (who * z.reg + j + 1) * LANES)
                 pb[p, :, lanes] = product(lanes).astype(BF16)
             send_x(p, j)
-        lanes = slice((z.tiles - 1) * LANES, z.tiles * LANES)
-        pb[p, :, lanes] = product(lanes).astype(BF16)
+        tile = product(slice((z.tiles - 1) * LANES, z.tiles * LANES)).astype(BF16)
+        for b in range(z.ns):
+            place = ((b % z.nx) * z.per + b // z.nx) * ROWS
+            pbl[p, place : place + ROWS, :] = tile[b * ROWS : (b + 1) * ROWS, :]
         send_x_last(p)
 
     def sum_x(p, j, extra=None):
         wait(rx.at[p, j], rx_r.at[p, j])
-        lanes = tile_lanes(xi, j) if j < z.reg else last
+        lanes = tile_lanes(xi, j)
         total = pb[p, :, lanes].astype(F32)
         for k in range(z.nx - 1):
             total += rx[p, j, k].astype(F32)
         if extra is not None:
-            total += extra(lanes)
+            total += extra(slice(None), lanes)
         sb[p, j] = total.astype(BF16)
 
+    def sum_x_last(p, extra=None):
+        wait(rxl.at[p], rx_r.at[p, z.reg])
+        total = pbl[p, share_rows(xi)].astype(F32)
+        for k in range(z.nx - 1):
+            total += rxl[p, k].astype(F32)
+        if extra is not None:
+            total += jnp.concatenate([extra(rows_of(member(xi, i)), last) for i in range(z.per)], axis=0)
+        sbl[p] = total.astype(BF16)
+
     def send_z(p, j):
-        if j < z.reg:
-            pltpu.make_async_copy(sb.at[p, j, rows_of(s)], zb.at[p, j, rows_of(s, zh * n)], zb_r.at[p, j]).start()
-        else:
-            pltpu.make_async_copy(
-                sb.at[p, j, rows_of(s)], ze.at[p, rows_of(s // z.nx, zh * z.per * ROWS)], zb_r.at[p, j]
-            ).start()
+        pltpu.make_async_copy(sb.at[p, j, rows_of(s)], zb.at[p, j, rows_of(s, zh * n)], zb_r.at[p, j]).start()
 
         def one(i, carry):
             to, dev = at_z(i)
-            dst = zb.at[p, j, rows_of(s, zh * n)] if j < z.reg else ze.at[p, rows_of(s // z.nx, zh * z.per * ROWS)]
-            send(sb.at[p, j, rows_of(to)], dst, zb_s.at[p, j], zb_r.at[p, j], dev)
+            send(sb.at[p, j, rows_of(to)], zb.at[p, j, rows_of(s, zh * n)], zb_s.at[p, j], zb_r.at[p, j], dev)
             return carry
 
         lax.fori_loop(2, 2 * z.ns + 1, one, 0)
-        leaving.append((zb, (p, 0, sent_z,), zb_s, (p, j,), None if j < z.reg else True))
+        leaving.append((zb, (p, 0, sent_z), zb_s, (p, j)))
+
+    def send_z_last(p):
+        dst = ze.at[p, rows_of(s // z.nx, zh * share)]
+        for i in range(z.per):
+            to = member(xi, i)
+            src = sbl.at[p, i * ROWS : (i + 1) * ROWS]
+            send(src, dst, zb_s.at[p, z.reg], zb_r.at[p, z.reg], (dp, to, (1 - zh) * z.nx + xi))
+
+            @pl.when(to != s)
+            def _():
+                send(src, dst, zb_s.at[p, z.reg], zb_r.at[p, z.reg], (dp, to, t))
+
+            @pl.when(to == s)
+            def _():
+                pltpu.make_async_copy(src, dst, zb_r.at[p, z.reg]).start()
+                pltpu.make_async_copy(src, spare.at[p], zb_s.at[p, z.reg]).start()
+
+        leaving.append((ze, (p,), zb_s, (p, z.reg)))
 
     def switch(p, extra=None):
         for j in range(z.reg):
             sum_x(p, j, extra)
             send_z(p, j)
-
-        @pl.when(is_owner)
-        def _():
-            sum_x(p, z.reg, extra)
-            send_z(p, z.reg)
+        sum_x_last(p, extra)
+        send_z_last(p)
 
     def sum_z(p, full, mine, others, extra=None):
         for j in range(z.reg):
@@ -280,22 +298,19 @@
             full[:, lanes] = total.astype(BF16)
             for k in range(z.nx - 1):
                 send(full.at[:, lanes], full.at[:, lanes], ag_s.at[p, j], ag_r.at[p, j, k], at_x(k))
-            leaving.append((rx, (p, j,), ag_s, (p, j,), None))
+            leaving.append((rx, (p, j), ag_s, (p, j)))
         wait(ze.at[p], zb_r.at[p, z.reg])
-        half = z.per * ROWS
-        for i in range(z.per):
-            total = ze[p, i * ROWS : (i + 1) * ROWS].astype(F32)
-            total += ze[p, half + i * ROWS : half + (i + 1) * ROWS].astype(F32)
-            if extra is not None:
-                total += extra[rows_of(xi + z.nx * i), last].astype(F32)
-            mine[i * ROWS : (i + 1) * ROWS, :] = total.astype(BF16)
+        total = ze[p, 0:share].astype(F32) + ze[p, share : 2 * share].astype(F32)
+        if extra is not None:
+            total += jnp.concatenate([extra[rows_of(member(xi, i)), last] for i in range(z.per)], axis=0).astype(F32)
+        mine[...] = total.astype(BF16)
         for k in range(z.nx - 1):
             send(mine, others.at[k], ag_s.at[p, z.reg], ag_r.at[p, z.reg, k], at_x(k))
-        leaving.append((others, (), ag_s, (p, z.reg,), None))
+        leaving.append((others, (), ag_s, (p, z.reg)))
 
     def place_last(full, block, who):
         for i in range(z.per):
-            full[rows_of(who + z.nx * i), last] = block[i * ROWS : (i + 1) * ROWS, :]
+            full[rows_of(member(who, i)), last] = block[i * ROWS : (i + 1) * ROWS, :]
 
     def gather_x(p, full, mine, others):
         place_last(full, mine, xi)
@@ -315,7 +330,7 @@
         placed = jnp.concatenate(
             [jnp.zeros((n, 3 * cols - base), BF16), mix_ref[...], jnp.zeros((n, z.wide - 4 * cols), BF16)], axis=1
         )
-        step = 192 if z.width % 192 == 0 else 160
+        step = z.width // 2
 
         def one(i, carry):
             at = pl.ds(pl.multiple_of(i * step, 16), step)
@@ -327,7 +342,7 @@
         lax.fori_loop(0, z.width // step, one, 0)
         away = pl.ds(pl.multiple_of((1 - core) * z.core_rows, 16), z.core_rows)
         send(term.at[b, away], term_in.at[b], w_s.at[b, 0], w_r.at[b, 0], (dp, s + 1 - 2 * core, t))
-        leaving.append((term_in, (b,), w_s, (b, 0,), None))
+        leaving.append((term_in, (b,), w_s, (b, 0,)))
 
     def weights_y(b):
         wait(term_in.at[b], w_r.at[b, 0])
@@ -337,7 +352,7 @@
             to = (dp + k + 1) % z.ny
             src = yb.at[b, pl.ds(pl.multiple_of(to * z.y_rows, 16), z.y_rows)]
             send(src, yr.at[b, k], w_s.at[b, 1], w_r.at[b, 1], (to, s, t))
-        leaving.append((yr, (b,), w_s, (b, 1,), None))
+        leaving.append((yr, (b,), w_s, (b, 1,)))
 
     def weights_z(b):
         wait(yr.at[b], w_r.at[b, 1])
@@ -355,7 +370,7 @@
         for k in range(z.nzl - 1):
             to = (zl + k + 1) % z.nzl
             send(zw.at[b, block(to)], zr.at[b, zl], w_s.at[b, 2], w_r.at[b, 2], (dp, 2 * to + core, t))
-        leaving.append((zr, (b, pl.ds(0, z.nzl - 1),), w_s, (b, 2,), None))
+        leaving.append((zr, (b, pl.ds(0, z.nzl - 1),), w_s, (b, 2,)))
 
     def weights_end(b, w_out):
         wait(zr.at[b], w_r.at[b, 2])
@@ -373,11 +388,12 @@
     loaded(3, 4)
     gm_s[...] = dot_nt(go_ref[...], wot_ref[...]).astype(BF16)
 
-    def add_input(lanes):
-        return x_ref[:, lanes].astype(F32) * jnp.where(zh == 0, 1.0, 0.0)
+    switch_heads(0, gm_s, gm_t)
+
+    def add_input(rows, lanes):
+        return x_ref[rows, lanes].astype(F32) * jnp.where(zh == 0, 1.0, 0.0)
 
     switch(0, add_input)
-    switch_heads(0, gm_s, gm_t)
     loaded(5)
     transposed(x_ref, lt_x)
     transposed(go_ref, lt_go)
@@ -420,46 +436,35 @@
     transposed(tg, lt_tg)
     weight_terms(1, lt_x, lt_tg, mix_s)
 
-    def exchange(j):
+    def exchange(src, dst, j):
+        send(src, dst, eb_s.at[j], eb_r.at[j], (dp, s, (1 - zh) * z.nx + xi))
+
+    for j in range(z.reg):
         sum_x(2, j)
-        send(sb.at[2, j], eb.at[j], eb_s.at[j], eb_r.at[j], (dp, s, (1 - zh) * z.nx + xi))
-        leaving.append((eb, (j,), eb_s, (j,), None if j < z.reg else True))
-
-    def finish(j, k_sem):
+        exchange(sb.at[2, j], eb.at[j], j)
+        leaving.append((eb, (j,), eb_s, (j,)))
+    sum_x_last(2)
+    exchange(sbl.at[2], ebl, z.reg)
+    leaving.append((ebl, (), eb_s, (z.reg,)))
+    weights_y(1)
+    for j in range(z.reg):
+        if j == 1:
+            weights_z(1)
         wait(eb.at[j], eb_r.at[j])
-        lanes = tile_lanes(xi, j) if j < z.reg else last
+        lanes = tile_lanes(xi, j)
         total = tg[:, lanes].astype(F32) + (sb[2, j].astype(F32) + eb[j].astype(F32))
         out_ref[:, lanes] = total.astype(BF16)
         for k in range(z.nx - 1):
-            send(out_ref.at[:, lanes], out_ref.at[:, lanes], ag_s.at[2, j], ag_r.at[2, j, k_sem(k)], at_x(k))
-        leaving.append((rx, (2, j,), ag_s, (2, j,), None if j < z.reg else True))
-
-    for j in range(z.reg):
-        exchange(j)
-
-    @pl.when(is_owner)
-    def _():
-        exchange(z.reg)
-
-    weights_y(1)
-    weights_z(1)
-    for j in range(z.reg):
-        finish(j, lambda k: k)
-
-    @pl.when(is_owner)
-    def _():
-        finish(z.reg, lambda k: 0)
-
+            send(out_ref.at[:, lanes], out_ref.at[:, lanes], ag_s.at[2, j], ag_r.at[2, j, k], at_x(k))
+        leaving.append((rx, (2, j), ag_s, (2, j)))
+    wait(ebl, eb_r.at[z.reg])
+    total = jnp.concatenate([tg[rows_of(member(xi, i)), last] for i in range(z.per)], axis=0).astype(F32)
+    oute[...] = (total + (sbl[2].astype(F32) + ebl[...].astype(F32))).astype(BF16)
+    for k in range(z.nx - 1):
+        send(oute, outg.at[k], ag_s.at[2, z.reg], ag_r.at[2, z.reg, k], at_x(k))
+    leaving.append((outg, (), ag_s, (2, z.reg)))
     weights_end(0, wt_out)
-    for k in range(z.nx - 1):
-        who = (xi - k - 1 + z.nx) % z.nx
-        for j in range(z.reg):
-            wait(out_ref.at[:, tile_lanes(who, j)], ag_r.at[2, j, k])
-
-    @pl.when(jnp.logical_not(is_owner))
-    def _():
-        wait(out_ref.at[:, last], ag_r.at[2, z.reg, 0])
-
+    gather_x(2, out_ref, oute, outg)
     weights_end(1, ws_out)
 
     on_leaving()
@@ -511,12 +516,13 @@
             vmem((n, cols), BF16), vmem((n, cols), BF16), vmem((n, cols), BF16),
             vmem((n, cols), BF16), vmem((n, cols), BF16),
             vmem((2, 3, n, cols), BF16),
-            vmem((3, n, width), BF16),
-            vmem((3, chunks, z.nx - 1, n, LANES), BF16),
-            vmem((3, chunks, n, LANES), BF16),
+            vmem((3, n, width), BF16), vmem((3, n, LANES), BF16),
+            vmem((3, z.reg, z.nx - 1, n, LANES), BF16), vmem((3, z.nx - 1, shared, LANES), BF16),
+            vmem((3, z.reg, n, LANES), BF16), vmem((3, shared, LANES), BF16),
             vmem((2, z.reg, 2 * n, LANES), BF16),
-            vmem((2, 2 * shared, LANES), BF16),
-            vmem((chunks, n, LANES), BF16),
+            vmem((2, 2 * shared, LANES), BF16), vmem((2, ROWS, LANES), BF16),
+            vmem((z.reg, n, LANES), BF16), vmem((shared, LANES), BF16),
+            vmem((shared, LANES), BF16), vmem((z.nx - 1, shared, LANES), BF16),
             vmem((n, width), BF16), vmem((shared, LANES), BF16), vmem((z.nx - 1, shared, LANES), BF16),
             vmem((n, width), BF16), vmem((shared, LANES), BF16), vmem((z.nx - 1, shared, LANES), BF16),
             vmem((width, n), BF16), vmem((width, n), BF16), vmem((width, n), BF16), vmem((width, n), BF16),

time: 112 us -> 112 us (level)
  no operation moved by 1% of the time
where the time goes in v4:
time: 112 us; the launch traced here: 110 us
  Pallas kernels  110 us (98%)
    pallas_call x1, Pallas kernels, run(): pl.pallas_call(functools.partial(kernel, z), out_shape=(jax.ShapeDtypeStr...  108 us

profile of v4, /device:TPU:6, one launch (start us, length us, event | category | flops | bytes accessed | tf_op | source)
XLA Modules:
  0.0 110.3 jit_solution(8594808738673542285)
XLA Ops:
  0.6 107.6 %shard_map.119 = (bf16[256,1152]{1,0:T(8,128)(2,1)}, f32[96,128]{1,0:T(8,128)}, f32[96,128]{1,0:T(8,128)}) custom-call(bf16[256,1152]{1,0:T(8,128)(2,1)} %bitcast.13, bf16[432,1152]{1,0:T(8,128)(2,1)} %bitcast.11, bf16[144,1152]{1,0:T(8,128)(2,1)} %wos_hbm.1, bf16[256,1152]{1,0:T(8,128)(2,1)} %bitcast.14, bf16[432,1152]{1,0:T(8,128)(2,1)} %bitcast.12, ...), custom_call_target="tpu_custom_call" | custom-call | tf_op jit(solution)/shard_map/pallas_call | solution.py:501
  108.2 2.1 %shard_map.120 = (bf16[256,1152]{1,0:T(8,128)(2,1)}, f32[18,3,144]{2,1,0:T(4,128)}, f32[18,144]{1,0:T(8,128)}, f32[18,3,144]{2,1,0:T(4,128)}, f32[18,144]{1,0:T(8,128)}) custom-call(bf16[256,1152]{1,0:T(8,128)(2,1)} %get-tuple-element.13.grad_ref, f32[96,128]{1,0:T(8,128)} %get-tuple-element.14.wt_ref, f32[96,128]{1,0:T(8,128)} %get-tuple-element.15.ws_ref), custom_call_target="tpu_custom_call" | custom-call | tf_op jit(solution)/shard_map/pallas_call | solution.py:487
